TPU v7x, 32 devices: a whole 2x2x4 slice. The times are simulated.
32 devices in a mesh: blk: 8 (over z, x), head: 2 (over y), dec: 2 (over core).
Axes of the slice: x: 2, y: 2, z: 4, core: 2. Of those that a mesh axis runs over, the one named last changes fastest.
Arguments:
- queries: bfloat16 [2048, 1536], P('blk', ('head', 'dec')), may hold values from -12 to 12
- key_vectors: bfloat16 [2048, 1536], P('blk', ('head', 'dec')), may hold values from -5 to 5
- values: bfloat16 [2048, 1536], P('blk', ('head', 'dec')), may hold values from -6 to 6
- lookback: int32 [12], replicated, may hold values from 0 to 5, as said below
- residual: bfloat16 [2048, 3072], P(('blk', 'head', 'dec')), may hold values from -0.1875 to 0.1875
- out_weight: bfloat16 [1536, 3072], P(('head', 'dec')), may hold values from -0.15625 to 0.15625
- branch_gate: float32 [3072], replicated, may hold values from 0.5 to 1.5
- final_shift: float32 [3072], replicated, may hold values from -0.5 to 0.5
- final_scale: float32 [3072], replicated, may hold values from -0.5 to 0.5
- final_weight: bfloat16 [3072, 64], replicated, may hold values from -0.109375 to 0.109375
- decoder_kernel: bfloat16 [432, 512], replicated, may hold values from -0.3125 to 0.3125
- decoder_bias: float32 [512], replicated, may hold values from -3 to 3
Outputs:
- features: bfloat16 [128, 64, 512], P(('blk', 'head', 'dec'))
Inputs may be any that keep to these rules, and one draw needn't show every extreme that they name: lookback[h] is how many frames before its own the queries of head h may see; some head sees 5 earlier frames and some head none.
All inputs are finite; a program needn't handle non-finite values.
Results may differ from a plain program's by a relative error of at most 0.02.
Values may be sent and summed in bfloat16 or wider, within the bound.
A program may use at most 192 MiB of HBM per device.

v0:
```python
import jax
import jax.numpy as jnp
from jax import lax
from jax.sharding import PartitionSpec as P

DH = 128
LC = 16
FRAMES = 8
PW = 32


def padded_2(cells, sides, width):
    for axis, dim in sides:
        count = lax.axis_size(axis)
        ends = count - 1
        head = lax.slice_in_dim(cells, 0, width, axis=dim)
        tail = lax.slice_in_dim(cells, cells.shape[dim] - width, cells.shape[dim], axis=dim)
        cells = jnp.concatenate(
            [
                lax.ppermute(tail, axis, [(i, (i + 1) % count) for i in range(ends)]),
                cells,
                lax.ppermute(head, axis, [((i + 1) % count, i) for i in range(ends)]),
            ],
            axis=dim,
        )
    return cells


def from_behind(x, axis, by):
    peers = lax.axis_size(axis)
    pairs = [(i, i + by) for i in range(peers) if 0 <= i + by < peers]
    return lax.ppermute(x, axis, pairs)


def attend_block(carry, shard_pair, query_heads, query_frame, lookback_heads, frame_len):
    running_max, row_total, accumulated = carry
    key_block, value_block = shard_pair
    key_count = key_block.shape[0]
    head_count = query_heads.shape[1]
    key_heads = key_block.reshape(key_count, head_count, DH)
    value_heads = value_block.reshape(key_count, head_count, DH)
    scores = jnp.einsum(
        "qhd,khd->hqk", query_heads, key_heads, preferred_element_type=jnp.float32
    ) * DH ** (-0.5)
    key_pos = jnp.arange(key_count, dtype=jnp.int32)
    key_frame = key_pos // frame_len
    visible = (
        (key_pos >= 0)[None, None, :]
        & (key_frame[None, None, :] <= query_frame[None, :, None])
        & (key_frame[None, None, :] >= query_frame[None, :, None] - lookback_heads[:, None, None])
    )
    masked = jnp.where(visible, scores, -1e30)
    newest_max = jnp.maximum(running_max, jnp.max(masked, axis=2))
    weights = jnp.where(visible, jnp.exp(scores - newest_max[:, :, None]), 0.0).astype(jnp.bfloat16)
    row_total = jnp.sum(weights.astype(jnp.float32), axis=2)
    accumulated = jnp.einsum(
        "hqk,khd->hqd", weights, value_heads, preferred_element_type=jnp.float32
    )
    return (newest_max, row_total, accumulated)


def per_device(
    queries,
    key_vectors,
    values,
    lookback,
    residual,
    out_weight,
    branch_gate,
    final_shift,
    final_scale,
    final_weight,
    decoder_kernel,
    decoder_bias,
):
    slab_rows = queries.shape[0]
    head_count = queries.shape[1] // DH
    blocks = lax.axis_size("blk")
    block_index = lax.axis_index("blk")
    frame_len = slab_rows * blocks // FRAMES
    query_heads = queries.reshape(slab_rows, head_count, DH)
    query_frame = (block_index * slab_rows + jnp.arange(slab_rows, dtype=jnp.int32)) // frame_len
    lookback_heads = lax.dynamic_slice_in_dim(
        lookback, lax.axis_index(("head", "dec")) * head_count, head_count
    )
    initial = (
        jnp.full((head_count, slab_rows), -1e30, jnp.float32),
        jnp.zeros((head_count, slab_rows), jnp.float32),
        jnp.zeros((head_count, slab_rows, DH), jnp.float32),
    )
    carry = attend_block(
        initial,
        (
            lax.all_gather(key_vectors, "blk", axis=0, tiled=True),
            lax.all_gather(values, "blk", axis=0, tiled=True),
        ),
        query_heads,
        query_frame,
        lookback_heads,
        frame_len,
    )
    newest_max, row_total, accumulated = carry
    attended = (
        (accumulated / row_total[:, :, None])
        .transpose(1, 0, 2)
        .reshape(slab_rows, head_count * DH)
        .astype(jnp.bfloat16)
    )
    tokens_dev = slab_rows // lax.axis_size(("head", "dec"))
    projected = lax.psum_scatter(
        jnp.dot(attended, out_weight, preferred_element_type=jnp.float32).astype(jnp.bfloat16),
        ("head", "dec"),
        scatter_dimension=0,
        tiled=True,
    ).astype(jnp.float32)
    hidden = residual.astype(jnp.float32) + branch_gate[None, :] * projected
    center = jnp.mean(hidden, axis=1, keepdims=True)
    spread = jnp.mean((hidden - center) ** 2, axis=1, keepdims=True)
    normed = (
        (hidden - center) * lax.rsqrt(spread + 1e-06) * (1.0 + final_scale[None, :])
        + final_shift[None, :]
    ).astype(jnp.bfloat16)
    patches = jnp.dot(normed, final_weight, preferred_element_type=jnp.float32).astype(jnp.bfloat16)
    patch_rows = tokens_dev // PW
    tile_rows = 2 * patch_rows
    width = 2 * PW
    tile = (
        patches.reshape(patch_rows, PW, 2, 2, LC)
        .transpose(0, 2, 1, 3, 4)
        .reshape(tile_rows, width * LC)
    )
    padded = padded_2(tile, ((("blk", "head", "dec"), 0),), 1)
    frame_stride = blocks // FRAMES
    frame_index = block_index // frame_stride
    prior_one = from_behind(padded, "blk", frame_stride)
    prior_one = jnp.where(frame_index >= 1, prior_one, padded)
    prior_two = from_behind(prior_one, "blk", frame_stride)
    prior_two = jnp.where(frame_index >= 1, prior_two, padded)
    history = jnp.stack([prior_two, prior_one, padded]).reshape(3, tile_rows + 2, width, LC)
    history = jnp.pad(history, ((0, 0), (0, 0), (1, 1), (0, 0)))
    windows = [
        history[time_tap, row_tap : row_tap + tile_rows, column_tap : column_tap + width, :]
        for time_tap in range(3)
        for row_tap in range(3)
        for column_tap in range(3)
    ]
    columns = jnp.concatenate(windows, axis=-1).reshape(tile_rows * width, 27 * LC)
    summed = (
        jnp.dot(columns, decoder_kernel, preferred_element_type=jnp.float32) + decoder_bias[None, :]
    )
    return summed.astype(jnp.bfloat16).reshape(tile_rows, width, decoder_kernel.shape[1])


def solution(mesh):
    in_specs = (
        P("blk", ("head", "dec")),
        P("blk", ("head", "dec")),
        P("blk", ("head", "dec")),
        P(),
        P(("blk", "head", "dec"), None),
        P(("head", "dec"), None),
        P(),
        P(),
        P(),
        P(),
        P(),
        P(),
    )
    out_specs = P(("blk", "head", "dec"), None, None)
    return jax.shard_map(
        per_device, mesh=mesh, in_specs=in_specs, out_specs=out_specs, check_vma=False
    )
```

profile of v0, /device:TPU:23, one launch (start us, length us, event | category | flops | bytes accessed | tf_op | source)
XLA Modules:
  0.0 178.1 jit_solution(16654968143980610500)
XLA Ops:
  6.5 1.9 %copy.25 = bf16[256,384]{0,1:T(8,128)(2,1)} copy(bf16[256,384]{1,0:T(8,128)(2,1)} %param.13) | data formatting | bytes 393216 | tf_op args[1]
  9.3 1.1 copy.24
  10.3 0.7 dynamic_slice.3
  11.5 41.9 %all-gather.3.cloned.1.call-done = bf16[2048,384]{0,1:T(8,128)(2,1)} async-done(((bf16[256,384]{0,1:T(8,128)(2,1)}), bf16[2048,384]{0,1:T(8,128)(2,1)}) %all-gather.3.cloned.1.call-update) | async-done | bytes 1572880 | tf_op jit(solution)/shard_map/all_gather | solution.py:94
  53.5 3.7 %select_reduce_fusion = (f32[3,256]{1,0:T(4,128)S(1)}, f32[3,256,2048]{2,1,0:T(8,128)S(1)}) fusion(s32[3,256]{1,0:T(4,128)S(1)} %broadcast_subtract_fusion, s32[2048]{0:T(1024)S(1)} %add_select_fusion, pred[256,2048]{1,0:T(8,128)(4,1)S(1)} %broadcast_compare_fusion, bf16[256,3,128]{0,2,1:T(8,128)(2,1)S(1)} %bitcast.81, bf16[2048,3,128]{0,2,1:T(8,128)(2,1)} %bitcast.84), kind=kOutput, calls=%fused_computation.2 | convolution fusion | flops 410516736 | bytes 8599552 | tf_op jit(solution)/shard_map/qhd,khd->hqk/dot_general | solution.py:42
  57.1 2.6 %copy-done.1 = f32[3,256,2048]{2,1,0:T(8,128)} copy-done((f32[3,256,2048]{2,1,0:T(8,128)}, f32[3,256,2048]{2,1,0:T(8,128)S(1)}, u32[]{:S(2)}) %copy-start.1) | copy-done | bytes 6291480
  59.8 2.4 %convert_reduce_fusion = f32[3,256]{1,0:T(4,128)S(1)} fusion(f32[3,256]{1,0:T(4,128)S(1)} %broadcast_maximum_fusion, f32[3,256,2048]{2,1,0:T(8,128)S(1)} %get-tuple-element.34, s32[3,256]{1,0:T(4,128)S(1)} %broadcast_subtract_fusion, s32[2048]{0:T(1024)S(1)} %add_select_fusion, pred[256,2048]{1,0:T(8,128)(4,1)S(1)} %broadcast_compare_fusion), kind=kLoop, calls=%fused_computation | loop fusion | flops 12582144 | bytes 6833152 | tf_op jit(solution)/shard_map/reduce_sum | solution.py:55
  62.2 36.5 %all-gather.5.cloned.1.call-done = bf16[2048,384]{1,0:T(8,128)(2,1)} async-done(((bf16[256,384]{1,0:T(8,128)(2,1)}), bf16[2048,384]{1,0:T(8,128)(2,1)}) %all-gather.5.cloned.1.call-update) | async-done | bytes 1572880 | tf_op jit(solution)/shard_map/all_gather | solution.py:95
  98.7 2.6 %copy.28 = bf16[2048,384]{0,1:T(8,128)(2,1)} copy(bf16[2048,384]{1,0:T(8,128)(2,1)} %all-gather.5.cloned.1.call-done) | data formatting | bytes 3145728 | tf_op jit(solution)/shard_map/all_gather | solution.py:95
  101.4 5.4 %fusion.2 = bf16[256,3,128]{0,2,1:T(8,128)(2,1)S(1)} fusion(bf16[2048,3,128]{0,2,1:T(8,128)(2,1)} %bitcast.51, f32[256,3]{0,1:T(4,128)S(1)} %bitcast.83, f32[3,256,2048]{2,1,0:T(8,128)} %copy-done.1, f32[3,256]{1,0:T(4,128)S(1)} %broadcast_maximum_fusion, s32[3,256]{1,0:T(4,128)S(1)} %broadcast_subtract_fusion, s32[2048]{0:T(1024)S(1)} %add_select_fusion, ...), kind=kOutput, calls=%fused_computation.9 | convolution fusion | flops 412286976 | bytes 8602624 | tf_op jit(solution)/shard_map/hqk,khd->hqd/dot_general | solution.py:56
  106.8 2.2 %convolution_convert_fusion = bf16[256,3072]{1,0:T(8,128)(2,1)} fusion(bf16[256,384]{0,1:T(8,128)(2,1)S(1)} %bitcast.80, bf16[384,3072]{1,0:T(8,128)(2,1)S(1)} %copy-done), kind=kOutput, calls=%fused_computation.4 | convolution fusion | flops 604766208 | bytes 4128768 | tf_op jit(solution)/shard_map/dot_general | solution.py:111
  109.0 27.8 %reduce-scatter.2.cloned.1.call-done = bf16[64,3072]{1,0:T(8,128)(2,1)} async-done(((bf16[256,3072]{1,0:T(8,128)(2,1)}), bf16[64,3072]{1,0:T(8,128)(2,1)}) %reduce-scatter.2.cloned.1.call-update) | async-done | bytes 393232 | tf_op jit(solution)/shard_map/reduce_scatter | solution.py:110
  136.8 1.2 fusion.3
  138.1 1.3 multiply_reduce_fusion
  139.4 1.4 convolution_convert_fusion.1
  141.2 4.6 %collective-permute-start = (bf16[1,1024]{1,0:T(2,128)(2,1)S(1)}, bf16[1,1024]{1,0:T(2,128)(2,1)S(1)}, u32[]{:S(2)}, u32[]{:S(2)}) collective-permute-start(bf16[1,1024]{1,0:T(2,128)(2,1)S(1)} %get-tuple-element.31), channel_id=1, source_target_pairs={{0,1},{1,2},{2,3},{3,4},{4,5},{5,6},{6,7},{7,8},{8,9},{9,10},{10,1... | collective-permute-start | bytes 6152 | tf_op jit(solution)/shard_map/ppermute | solution.py:20
  145.8 1.9 %collective-permute-start.1 = (bf16[1,1024]{1,0:T(2,128)(2,1)S(1)}, bf16[1,1024]{1,0:T(2,128)(2,1)S(1)}, u32[]{:S(2)}, u32[]{:S(2)}) collective-permute-start(bf16[1,1024]{1,0:T(2,128)(2,1)S(1)} %get-tuple-element.32), channel_id=1, source_target_pairs={{1,0},{2,1},{3,2},{4,3},{5,4},{6,5},{7,6},{8,7},{9,8},{10,9},{11,1... | collective-permute-start | bytes 6152 | tf_op jit(solution)/shard_map/ppermute | solution.py:22
  148.0 4.5 %collective-permute-done.1 = bf16[1,1024]{1,0:T(2,128)(2,1)S(1)} collective-permute-done((bf16[1,1024]{1,0:T(2,128)(2,1)S(1)}, bf16[1,1024]{1,0:T(2,128)(2,1)S(1)}, u32[]{:S(2)}, u32[]{:S(2)}) %collective-permute-start.1) | collective-permute-done | bytes 2080 | tf_op jit(solution)/shard_map/ppermute | solution.py:22
  152.7 2.2 %collective-permute-start.2 = (bf16[6,1024]{1,0:T(8,128)(2,1)S(1)}, bf16[6,1024]{1,0:T(8,128)(2,1)S(1)}, u32[]{:S(2)}, u32[]{:S(2)}) collective-permute-start(bf16[6,1024]{1,0:T(8,128)(2,1)S(1)} %pad_maximum_fusion.2), channel_id=1, source_target_pairs={{0,4},{4,8},{8,12},{12,16},{16,20},{20,24},{24,28},{1,5},{5,9},{9,... | collective-permute-start | bytes 36872 | tf_op jit(solution)/shard_map/ppermute | solution.py:32
  155.2 2.0 %collective-permute-done.2 = bf16[6,1024]{1,0:T(8,128)(2,1)S(1)} collective-permute-done((bf16[6,1024]{1,0:T(8,128)(2,1)S(1)}, bf16[6,1024]{1,0:T(8,128)(2,1)S(1)}, u32[]{:S(2)}, u32[]{:S(2)}) %collective-permute-start.2) | collective-permute-done | bytes 12320 | tf_op jit(solution)/shard_map/ppermute | solution.py:32
  157.2 3.1 %collective-permute-start.3 = (bf16[6,1024]{1,0:T(8,128)(2,1)S(1)}, bf16[6,1024]{1,0:T(8,128)(2,1)S(1)}, u32[]{:S(2)}, u32[]{:S(2)}) collective-permute-start(bf16[6,1024]{1,0:T(8,128)(2,1)S(1)} %broadcast_select_fusion.1), channel_id=1, source_target_pairs={{0,4},{4,8},{8,12},{12,16},{16,20},{20,24},{24,28},{1,5},{5,9},{9,... | collective-permute-start | bytes 36872 | tf_op jit(solution)/shard_map/ppermute | solution.py:32
  166.5 0.7 copy.37
  167.3 2.2 %concatenate.111 = bf16[256,432]{1,0:T(8,128)(2,1)} concatenate(bf16[256,16]{1,0:T(8,128)(2,1)} %bitcast.73, bf16[256,16]{1,0:T(8,128)(2,1)} %bitcast.79, bf16[256,16]{1,0:T(8,128)(2,1)S(1)} %bitcast.56, bf16[256,16]{1,0:T(8,128)(2,1)S(1)} %bitcast.57, bf16[256,16]{1,0:T(8,128)(2,1)} %bitcast.78, bf16[256,16]{1,0:T(8,128)(2,1)S(1)} %bitcast.58, bf16[256,16]{1,0:T(8,128)(2,1)S(1)} %bitcast.59, ...), dimensions={1} | concatenate | bytes 442368 | tf_op jit(solution)/shard_map/concatenate | solution.py:147
  169.5 2.1 %fusion = bf16[256,512]{1,0:T(8,128)(2,1)} fusion(bf16[256,432]{1,0:T(8,128)(2,1)} %concatenate.111, bf16[432,512]{1,0:T(8,128)(2,1)} %param.22, f32[512]{0:T(512)} %param.23), kind=kOutput, calls=%fused_computation.6 | convolution fusion | flops 113508352 | bytes 927744 | tf_op jit(solution)/shard_map/dot_general | solution.py:149
  (72 shorter events, 8.6 us)
Async XLA Ops:
  6.5 100.3 %copy-start = (bf16[384,3072]{1,0:T(8,128)(2,1)S(1)}, bf16[384,3072]{1,0:T(8,128)(2,1)}, u32[]{:S(2)}) copy-start(bf16[384,3072]{1,0:T(8,128)(2,1)} %param.17) | copy-start | bytes 7077892
  6.5 46.9 %all-gather.3.cloned.1.call-start = ((), (), s32[]{:S(2)}) async-start(), calls=%async_computation.1 | async-start | bytes 1769472 | tf_op jit(solution)/shard_map/all_gather | solution.py:94
  8.5 90.3 %all-gather.5.cloned.1.call-start = ((), (), s32[]{:S(2)}) async-start(), calls=%async_computation.2 | async-start | bytes 1769472 | tf_op jit(solution)/shard_map/all_gather | solution.py:95
  9.2 127.6 %reduce-scatter.2.cloned.1.call-start = ((), (), s32[]{:S(2)}) async-start(), calls=%async_computation.3 | async-start | bytes 1966080 | tf_op jit(solution)/shard_map/reduce_scatter | solution.py:110
  57.1 2.7 %copy-start.1 = (f32[3,256,2048]{2,1,0:T(8,128)}, f32[3,256,2048]{2,1,0:T(8,128)S(1)}, u32[]{:S(2)}) copy-start(f32[3,256,2048]{2,1,0:T(8,128)S(1)} %get-tuple-element.34) | copy-start | bytes 18874372
  101.4 7.6 %copy-start.4 = (f32[3072]{0:T(1024)S(1)}, f32[3072]{0:T(1024)}, u32[]{:S(2)}) copy-start(f32[3072]{0:T(1024)} %param.20) | copy-start | bytes 36868
  101.4 35.5 %copy-start.2 = (bf16[64,3072]{1,0:T(8,128)(2,1)S(1)}, bf16[64,3072]{1,0:T(8,128)(2,1)}, u32[]{:S(2)}) copy-start(bf16[64,3072]{1,0:T(8,128)(2,1)} %param.16) | copy-start | bytes 1179652
  101.4 35.5 %copy-start.3 = (f32[3072]{0:T(1024)S(1)}, f32[3072]{0:T(1024)}, u32[]{:S(2)}) copy-start(f32[3072]{0:T(1024)} %param.18) | copy-start | bytes 36868
  106.8 32.6 %copy-start.5 = (bf16[3072,64]{0,1:T(8,128)(2,1)S(1)}, bf16[3072,64]{0,1:T(8,128)(2,1)}, u32[]{:S(2)}) copy-start(bf16[3072,64]{0,1:T(8,128)(2,1)} %param.21) | copy-start | bytes 1179652
  106.8 32.6 %copy-start.6 = (f32[3072]{0:T(1024)S(1)}, f32[3072]{0:T(1024)}, u32[]{:S(2)}) copy-start(f32[3072]{0:T(1024)} %param.19) | copy-start | bytes 36868
  141.2 6.6 %collective-permute-start = (bf16[1,1024]{1,0:T(2,128)(2,1)S(1)}, bf16[1,1024]{1,0:T(2,128)(2,1)S(1)}, u32[]{:S(2)}, u32[]{:S(2)}) collective-permute-start(bf16[1,1024]{1,0:T(2,128)(2,1)S(1)} %get-tuple-element.31), channel_id=1, source_target_pairs={{0,1},{1,2},{2,3},{3,4},{4,5},{5,6},{6,7},{7,8},{8,9},{9,10},{10,1... | collective-permute-start | bytes 6152 | tf_op jit(solution)/shard_map/ppermute | solution.py:20
  145.8 6.7 %collective-permute-start.1 = (bf16[1,1024]{1,0:T(2,128)(2,1)S(1)}, bf16[1,1024]{1,0:T(2,128)(2,1)S(1)}, u32[]{:S(2)}, u32[]{:S(2)}) collective-permute-start(bf16[1,1024]{1,0:T(2,128)(2,1)S(1)} %get-tuple-element.32), channel_id=1, source_target_pairs={{1,0},{2,1},{3,2},{4,3},{5,4},{6,5},{7,6},{8,7},{9,8},{10,9},{11,1... | collective-permute-start | bytes 6152 | tf_op jit(solution)/shard_map/ppermute | solution.py:22
  152.7 4.5 %collective-permute-start.2 = (bf16[6,1024]{1,0:T(8,128)(2,1)S(1)}, bf16[6,1024]{1,0:T(8,128)(2,1)S(1)}, u32[]{:S(2)}, u32[]{:S(2)}) collective-permute-start(bf16[6,1024]{1,0:T(8,128)(2,1)S(1)} %pad_maximum_fusion.2), channel_id=1, source_target_pairs={{0,4},{4,8},{8,12},{12,16},{16,20},{20,24},{24,28},{1,5},{5,9},{9,... | collective-permute-start | bytes 36872 | tf_op jit(solution)/shard_map/ppermute | solution.py:32
  157.2 4.5 %collective-permute-start.3 = (bf16[6,1024]{1,0:T(8,128)(2,1)S(1)}, bf16[6,1024]{1,0:T(8,128)(2,1)S(1)}, u32[]{:S(2)}, u32[]{:S(2)}) collective-permute-start(bf16[6,1024]{1,0:T(8,128)(2,1)S(1)} %broadcast_select_fusion.1), channel_id=1, source_target_pairs={{0,4},{4,8},{8,12},{12,16},{16,20},{20,24},{24,28},{1,5},{5,9},{9,... | collective-permute-start | bytes 36872 | tf_op jit(solution)/shard_map/ppermute | solution.py:32
Sparse Core Ops, SparseCore 0:
  9.4 44.0 all-gather.2
  55.6 43.0 all-gather.4
  109.1 27.6 reduce-scatter.1
where the time goes:
time: 181 us; the launch traced here: 178 us
  waiting for transfers between devices  114 us (63%)
  local copies, waits for them, and re-layouts  18.5 us (10%)
  matrix products  14.7 us (8%)
  between operations  13.4 us (7%)
  starting transfers between devices  11.9 us (7%)
  other arithmetic  5.65 us (3%)
    all_gather x1, waiting for transfers between devices, per_device(): lax.all_gather(key_vectors, 'blk', axis=0, tiled=True)  41.9 us
    all_gather x1, waiting for transfers between devices, per_device(): lax.all_gather(values, 'blk', axis=0, tiled=True)  36.5 us
    reduce_scatter x1, waiting for transfers between devices, per_device(): lax.psum_scatter(jnp.dot(attended, out_weight, preferred_element_type=jnp...  27.8 us
    slice x23, local copies, waits for them, and re-layouts, per_device(): history[time_tap, row_tap:row_tap + tile_rows, column_tap:column_tap + wi...  6.06 us
    unnamed x16, local copies, waits for them, and re-layouts  5.62 us
    dot_general x1, matrix products, attend_block(): jnp.einsum('hqk,khd->hqd', weights, value_heads, preferred_element_type=j...  5.39 us
    ppermute x2, starting transfers between devices, from_behind(): return lax.ppermute(x, axis, pairs)  5.3 us
    ppermute x1, starting transfers between devices, padded_2(): lax.ppermute(tail, axis, [(i, (i + 1) % count) for i in range(ends)])  4.56 us
  transfers between devices with their start and end apart: 7, of which 6 were waited for; matrix products, arithmetic and copies ran while one was open for 5% of the time, Pallas kernels for 0%

commit v1 on v0

--- a/solution.py
+++ b/solution.py
@@ -1,6 +1,8 @@
 import jax
 import jax.numpy as jnp
 from jax import lax
+from jax.experimental import pallas as pl
+from jax.experimental.pallas import tpu as pltpu
 from jax.sharding import PartitionSpec as P
 
 DH = 128
@@ -151,6 +153,334 @@
     return summed.astype(jnp.bfloat16).reshape(tile_rows, width, decoder_kernel.shape[1])
 
 
+HIGH = 3
+CHUNKS = 4
+MESH = pl.DeviceIdType.MESH
+
+
+def fused_kernel(
+    q_hbm, k_hbm, v_hbm, lookback, res_hbm, w_hbm, gate_hbm, shift_hbm, scale_hbm, fw_hbm, dk_hbm, db_hbm,
+    out_ref,
+    kz, kx, qv, wv, resv, gatev, shiftv, scalev, fwv, dkv, dbv,
+    top, total, acc, att, part, from_dec, to_y, from_y, hid, halo, wide, canvas,
+    load_sem, kv_sem, zs, zr, xs, xr, ds, dr, ys, yr, hs, hr,
+):
+    f = lax.axis_index("blk")
+    hd = lax.axis_index("head")
+    dc = lax.axis_index("dec")
+    z, x = f // 2, f % 2
+    n = f * 4 + hd * 2 + dc
+    slab = q_hbm.shape[0]
+    columns = w_hbm.shape[1] // CHUNKS
+
+    kv_loads = []
+    for h in range(HIGH):
+        for which, src in enumerate((k_hbm, v_hbm)):
+            kv_loads.append(
+                pltpu.make_async_copy(
+                    src.at[:, pl.ds(h * DH, DH)], kz.at[0, h, which], kv_sem.at[2 * h + which]
+                )
+            )
+    loads = [
+        pltpu.make_async_copy(src, dst, load_sem.at[i])
+        for i, (src, dst) in enumerate(
+            (
+                (q_hbm, qv), (dk_hbm, dkv), (w_hbm, wv), (res_hbm, resv), (gate_hbm, gatev),
+                (shift_hbm, shiftv), (scale_hbm, scalev), (fw_hbm, fwv), (db_hbm, dbv),
+            )
+        )
+    ]
+    for c in kv_loads + loads:
+        c.start()
+
+    def up(j, h):
+        return pltpu.make_async_remote_copy(
+            src_ref=kz.at[j, h], dst_ref=kz.at[j + 1, h], send_sem=zs.at[j, h], recv_sem=zr.at[j + 1, h],
+            device_id=(f + 2, hd, dc), device_id_type=MESH,
+        )
+
+    def across(j, h):
+        return pltpu.make_async_remote_copy(
+            src_ref=kz.at[j + x, h], dst_ref=kx.at[j, h], send_sem=xs.at[j, h], recv_sem=xr.at[j, h],
+            device_id=(f + 1 - 2 * x, hd, dc), device_id_type=MESH,
+        )
+
+    def up_goes(j):
+        return (z >= j) & (z < 3) & ((x == 1) | (j < 2))
+
+    def up_comes(j):
+        return (z >= j) & ((x == 1) | (j < 3))
+
+    def across_goes(j):
+        return z >= j + x
+
+    def across_comes(j):
+        return z >= j + 1 - x
+
+    for h in range(HIGH):
+        kv_loads[2 * h].wait()
+        kv_loads[2 * h + 1].wait()
+
+        @pl.when(up_goes(0))
+        def _():
+            up(0, h).start()
+
+        @pl.when(x == 0)
+        def _():
+            across(0, h).start()
+
+    def attend(h, key, value, distance):
+        query = qv[:, h * DH : (h + 1) * DH]
+        scores = lax.dot_general(
+            query, key, (((1,), (1,)), ((), ())), preferred_element_type=jnp.float32
+        ) * DH ** (-0.5)
+        if distance == 0:
+            newest = jnp.max(scores, axis=1, keepdims=True)
+        else:
+            seen = lookback[(hd * 2 + dc) * HIGH + h] >= distance
+            scores = scores + jnp.where(seen, 0.0, -1e30)
+            newest = jnp.maximum(top[h], jnp.max(scores, axis=1, keepdims=True))
+        weights = jnp.exp(scores - newest).astype(jnp.bfloat16)
+        added = jnp.sum(weights.astype(jnp.float32), axis=1, keepdims=True)
+        mixed = jnp.dot(weights, value, preferred_element_type=jnp.float32)
+        if distance == 0:
+            total[h] = added
+            acc[h] = mixed
+        else:
+            shrink = jnp.exp(top[h] - newest)
+            total[h] = total[h] * shrink + added
+            acc[h] = acc[h] * shrink + mixed
+        top[h] = newest
+
+    loads[0].wait()
+    for h in range(HIGH):
+        attend(h, kz[0, h, 0], kz[0, h, 1], 0)
+
+    loads[1].wait()
+    wide[...] = jnp.zeros_like(wide)
+    for a in range(2):
+        for b in range(2):
+            for t in range(3):
+                for i in range(3):
+                    for j in range(3):
+                        ya, xb = a + i - 1, b + j - 1
+                        row = ((t * 2 + ya // 2 - (a - 1)) * 2 + xb // 2 - (b - 1)) * 64
+                        row += ((ya % 2) * 2 + xb % 2) * LC
+                        tap = (t * 3 + i) * 3 + j
+                        wide[a * 2 + b, row : row + LC, :] = dkv[tap * LC : (tap + 1) * LC, :]
+
+    def z_part(j, h):
+        @pl.when(up_comes(j))
+        def _():
+            up(j - 1, h).wait_recv()
+            if j <= 2:
+
+                @pl.when(up_goes(j))
+                def _():
+                    up(j, h).start()
+
+                @pl.when(x == 0)
+                def _():
+                    across(j, h).start()
+
+            @pl.when(x == 1)
+            def _():
+                across(j - 1, h).start()
+
+            if j <= 2:
+                attend(h, kz[j, h, 0], kz[j, h, 1], 2 * j)
+
+    def x_part(j, h):
+        @pl.when(across_comes(j))
+        def _():
+            across(j, h).wait_recv()
+            attend(h, kx[j, h, 0], kx[j, h, 1], 2 * j + 1)
+
+    order = [(j, h) for j in range(1, 4) for h in range(HIGH)]
+    for place, (j, h) in enumerate(order):
+        z_part(j, h)
+        if place:
+            x_part(order[place - 1][0] - 1, order[place - 1][1])
+    x_part(order[-1][0] - 1, order[-1][1])
+
+    for h in range(HIGH):
+        att[:, h * DH : (h + 1) * DH] = (acc[h] / total[h]).astype(jnp.bfloat16)
+
+    def to_core(c):
+        return pltpu.make_async_remote_copy(
+            src_ref=part.at[c, :, 1 - dc], dst_ref=from_dec.at[c], send_sem=ds.at[c], recv_sem=dr.at[c],
+            device_id=(f, hd, 1 - dc), device_id_type=MESH,
+        )
+
+    def to_row(c):
+        return pltpu.make_async_remote_copy(
+            src_ref=to_y.at[c], dst_ref=from_y.at[c], send_sem=ys.at[c], recv_sem=yr.at[c],
+            device_id=(f, 1 - hd, dc), device_id_type=MESH,
+        )
+
+    loads[2].wait()
+    for c in range(CHUNKS):
+        share = jnp.dot(
+            att[...], wv[:, c * columns : (c + 1) * columns], preferred_element_type=jnp.float32
+        ).astype(jnp.bfloat16)
+        part[c] = share.reshape(2, 2, slab // 4, columns)
+        to_core(c).start()
+    for c in range(CHUNKS):
+        to_core(c).wait_recv()
+        to_y[c] = (
+            part[c, 1 - hd, dc].astype(jnp.float32) + from_dec[c, 1 - hd].astype(jnp.float32)
+        ).astype(jnp.bfloat16)
+        to_row(c).start()
+    for load in loads[3:]:
+        load.wait()
+    summed = jnp.zeros((slab // 4, 1), jnp.float32)
+    for c in range(CHUNKS):
+        cols = slice(c * columns, (c + 1) * columns)
+        mine = part[c, hd, dc].astype(jnp.float32) + from_dec[c, hd].astype(jnp.float32)
+        to_row(c).wait_recv()
+        hidden = resv[:, cols].astype(jnp.float32) + gatev[:, cols] * (mine + from_y[c].astype(jnp.float32))
+        hid[c] = hidden
+        summed = summed + jnp.sum(hidden, axis=1, keepdims=True)
+    center = summed / (CHUNKS * columns)
+    squares = jnp.zeros((slab // 4, 1), jnp.float32)
+    for c in range(CHUNKS):
+        squares = squares + jnp.sum((hid[c] - center) ** 2, axis=1, keepdims=True)
+    inverse = lax.rsqrt(squares / (CHUNKS * columns) + 1e-06)
+    patches = jnp.zeros((slab // 4, fwv.shape[1]), jnp.float32)
+    for c in range(CHUNKS):
+        cols = slice(c * columns, (c + 1) * columns)
+        normed = ((hid[c] - center) * inverse * (1.0 + scalev[:, cols]) + shiftv[:, cols]).astype(jnp.bfloat16)
+        patches = patches + jnp.dot(normed, fwv[cols, :], preferred_element_type=jnp.float32)
+    halo[0, 1] = jnp.concatenate([patches, patches], axis=1).astype(jnp.bfloat16)
+
+    def tile_to(back, side):
+        m = n + 4 * back - side
+        copy = pltpu.make_async_remote_copy(
+            src_ref=halo.at[0, 1], dst_ref=halo.at[back, side + 1],
+            send_sem=hs.at[back, side + 1], recv_sem=hr.at[back, side + 1],
+            device_id=(m // 4, (m % 4) // 2, m % 2), device_id_type=MESH,
+        )
+        return copy, (m >= 4 * back) & (m < 32)
+
+    def tile_comes(back, side):
+        source = n - 4 * back + side
+        return (f >= back) & (source >= 0) & (source < 32)
+
+    reach = [(back, side) for back in (2, 1, 0) for side in (-1, 0, 1) if (back, side) != (0, 0)]
+    for back, side in reach:
+        copy, goes = tile_to(back, side)
+
+        @pl.when(goes)
+        def _():
+            copy.start()
+
+    for back, side in reach:
+
+        @pl.when(tile_comes(back, side))
+        def _():
+            tile_to(back, side)[0].wait_recv()
+
+    rows = 4 * PW
+    lane = lax.broadcasted_iota(jnp.int32, (rows, 128), 1)
+    token = lax.broadcasted_iota(jnp.int32, (rows, 128), 0) % PW
+    pairs = []
+    for t in range(3):
+        back = jnp.minimum(2 - t, f)
+        first = n - 4 * back
+        above = jnp.where(first >= 1, halo[back, 0, PW:, :].astype(jnp.float32), 0.0)
+        below = jnp.where(first <= 30, halo[back, 2, :PW, :].astype(jnp.float32), 0.0)
+        ext = jnp.concatenate([above, halo[back, 1].astype(jnp.float32), below], axis=0)
+        before = jnp.where(token == 0, 0.0, pltpu.roll(ext, 1, 0))
+        after = jnp.where(token == PW - 1, 0.0, pltpu.roll(ext, rows - 1, 0))
+        pairs.append(
+            (
+                jnp.where(lane < 64, before, ext).astype(jnp.bfloat16),
+                jnp.where(lane < 64, ext, after).astype(jnp.bfloat16),
+            )
+        )
+    for a in range(2):
+        for b in range(2):
+            lhs = jnp.concatenate(
+                [
+                    pairs[t][b][(a + d) * PW : (a + d) * PW + 2 * PW]
+                    for t in range(3)
+                    for d in range(2)
+                ],
+                axis=1,
+            )
+            got = jnp.dot(lhs, wide[a * 2 + b], preferred_element_type=jnp.float32) + dbv[...]
+            for r in range(2):
+                for g in range(got.shape[1] // 128):
+                    canvas[g, pl.ds((2 * r + a) * 2 * PW + b, PW, stride=2), :] = got[
+                        r * PW : (r + 1) * PW, g * 128 : (g + 1) * 128
+                    ]
+    for y in range(4):
+        for g in range(canvas.shape[0]):
+            out_ref[y, :, g * 128 : (g + 1) * 128] = canvas[g, y * 2 * PW : (y + 1) * 2 * PW, :].astype(jnp.bfloat16)
+
+    for j in range(3):
+        for h in range(HIGH):
+
+            @pl.when(up_goes(j))
+            def _():
+                up(j, h).wait_send()
+
+            @pl.when(across_goes(j))
+            def _():
+                across(j, h).wait_send()
+
+    for c in range(CHUNKS):
+        to_core(c).wait_send()
+        to_row(c).wait_send()
+    for back, side in reach:
+        copy, goes = tile_to(back, side)
+
+        @pl.when(goes)
+        def _():
+            copy.wait_send()
+
+
+def fused(
+    queries, key_vectors, values, lookback, residual, out_weight,
+    branch_gate, final_shift, final_scale, final_weight, decoder_kernel, decoder_bias,
+):
+    slab, width = queries.shape
+    model = out_weight.shape[1]
+    quarter, columns = slab // 4, model // CHUNKS
+    outputs = decoder_kernel.shape[1]
+    bf, f32 = jnp.bfloat16, jnp.float32
+    vm, dma = pltpu.VMEM, pltpu.SemaphoreType.DMA
+    hbm = pl.BlockSpec(memory_space=pl.ANY)
+    return pl.pallas_call(
+        fused_kernel,
+        out_shape=jax.ShapeDtypeStruct((4, 2 * PW, outputs), bf),
+        in_specs=[hbm] * 3 + [pl.BlockSpec(memory_space=pltpu.SMEM)] + [hbm] * 8,
+        out_specs=pl.BlockSpec(memory_space=pltpu.VMEM),
+        scratch_shapes=[
+            vm((4, HIGH, 2, slab, DH), bf), vm((3, HIGH, 2, slab, DH), bf), vm((slab, width), bf),
+            vm((width, model), bf), vm((quarter, model), bf),
+            vm((1, model), f32), vm((1, model), f32), vm((1, model), f32),
+            vm(final_weight.shape, bf), vm(decoder_kernel.shape, bf), vm((1, outputs), f32),
+            vm((HIGH, slab, 1), f32), vm((HIGH, slab, 1), f32), vm((HIGH, slab, DH), f32),
+            vm((slab, width), bf), vm((CHUNKS, 2, 2, quarter, columns), bf),
+            vm((CHUNKS, 2, quarter, columns), bf), vm((CHUNKS, quarter, columns), bf),
+            vm((CHUNKS, quarter, columns), bf), vm((CHUNKS, quarter, columns), f32),
+            vm((3, 3, quarter, 128), bf), vm((4, 768, outputs), bf), vm((outputs // 128, 256, 128), f32),
+            dma((9,)), dma((6,)), dma((3, HIGH)), dma((4, HIGH)), dma((3, HIGH)), dma((3, HIGH)),
+            dma((CHUNKS,)), dma((CHUNKS,)), dma((CHUNKS,)), dma((CHUNKS,)), dma((3, 3)), dma((3, 3)),
+        ],
+        compiler_params=pltpu.CompilerParams(has_side_effects=True, vmem_limit_bytes=48 * 1024 * 1024),
+    )(
+        queries, key_vectors, values, lookback, residual, out_weight,
+        branch_gate.reshape(1, -1), final_shift.reshape(1, -1), final_scale.reshape(1, -1),
+        final_weight, decoder_kernel, decoder_bias.reshape(1, -1),
+    )
+
+
+def one_slab_a_frame(mesh):
+    return (mesh.shape["blk"], mesh.shape["head"], mesh.shape["dec"]) == (FRAMES, 2, 2)
+
+
 def solution(mesh):
     in_specs = (
         P("blk", ("head", "dec")),
@@ -167,6 +497,7 @@
         P(),
     )
     out_specs = P(("blk", "head", "dec"), None, None)
+    body = fused if one_slab_a_frame(mesh) else per_device
     return jax.shard_map(
-        per_device, mesh=mesh, in_specs=in_specs, out_specs=out_specs, check_vma=False
-    )
+        body, mesh=mesh, in_specs=in_specs, out_specs=out_specs, check_vma=False
+    )

time: 181 us -> 71 us (0.39); the launches traced: 178 us -> 70.5 us
  waiting for transfers between devices: 114 us -> 0 us
  Pallas kernels: 0 us -> 58.5 us
  matrix products: 14.7 us -> 0 us
  between operations: 13.4 us -> 0.04 us
  starting transfers between devices: 11.9 us -> 0 us
  local copies, waits for them, and re-layouts: 18.5 us -> 12 us
  other arithmetic: 5.65 us -> 0 us
    all_gather x2 -> x0, waiting for transfers between devices: 78.5 us -> none  [the longest x1 41.9 us: per_device(): lax.all_gather(key_vectors, 'blk', axis=0, tiled=True)]
    pallas_call x0 -> x1, Pallas kernels: none -> 58.5 us  [fused(): pl.pallas_call(fused_kernel, out_shape=jax.ShapeDtypeStruct((4, 2 * PW, o...]
    reduce_scatter x1 -> x0, waiting for transfers between devices: 27.8 us -> none  [per_device(): lax.psum_scatter(jnp.dot(attended, out_weight, preferred_element_type=jnp...]
    dot_general x5 -> x0, matrix products: 14.7 us -> none  [the longest x1 5.39 us: attend_block(): jnp.einsum('hqk,khd->hqd', weights, value_heads, preferred_element_type=j...]
    ppermute x4 -> x0, starting transfers between devices: 11.8 us -> none  [the longest x2 5.3 us: from_behind(): return lax.ppermute(x, axis, pairs)]
    ppermute x4 -> x0, waiting for transfers between devices: 7.01 us -> none  [the longest x1 4.51 us: padded_2(): lax.ppermute(head, axis, [((i + 1) % count, i) for i in range(ends)])]
    unnamed x16 -> x24, local copies, waits for them, and re-layouts: 5.62 us -> 12 us
    slice x24 -> x0, local copies, waits for them, and re-layouts: 6.07 us -> none  [the longest x23 6.06 us: per_device(): history[time_tap, row_tap:row_tap + tile_rows, column_tap:column_tap + wi...]
  transfers between devices with their start and end apart: 7 -> 0, of which waited for: 6 -> 0; matrix products, arithmetic and copies ran while one was open for 5% -> 0% of each run, Pallas kernels for 0% -> 0%
where the time goes in v1:
time: 71 us; the launch traced here: 70.5 us
  Pallas kernels  58.5 us (82%)
  local copies, waits for them, and re-layouts  12 us (17%)
    pallas_call x1, Pallas kernels, fused(): pl.pallas_call(fused_kernel, out_shape=jax.ShapeDtypeStruct((4, 2 * PW, o...  58.5 us
    unnamed x24, local copies, waits for them, and re-layouts  12 us

profile of v1, /device:TPU:23, one launch (start us, length us, event | category | flops | bytes accessed | tf_op | source)
XLA Modules:
  0.0 70.5 jit_solution(7629810959969535098)
XLA Ops:
  0.0 1.4 %copy.13.fw_hbm = bf16[3072,64]{1,0:T(8,128)(2,1)S(1)} copy(bf16[3072,64]{0,1:T(8,128)(2,1)} %param.21) | data formatting | bytes 786432 | tf_op args[9]
  1.4 0.0 copy-start
  1.4 1.7 %copy-done = bf16[384,3072]{1,0:T(8,128)(2,1)S(1)} copy-done((bf16[384,3072]{1,0:T(8,128)(2,1)S(1)}, bf16[384,3072]{1,0:T(8,128)(2,1)}, u32[]{:S(2)}) %copy-start) | copy-done | bytes 2359320
  3.0 0.0 copy-start.1
  3.0 1.0 %copy-done.1 = bf16[432,512]{1,0:T(8,128)(2,1)S(1)} copy-done((bf16[432,512]{1,0:T(8,128)(2,1)S(1)}, bf16[432,512]{1,0:T(8,128)(2,1)}, u32[]{:S(2)}) %copy-start.1) | copy-done | bytes 442392
  4.1 0.0 copy-start.2
  4.1 1.0 %copy-done.2 = bf16[64,3072]{1,0:T(8,128)(2,1)S(1)} copy-done((bf16[64,3072]{1,0:T(8,128)(2,1)S(1)}, bf16[64,3072]{1,0:T(8,128)(2,1)}, u32[]{:S(2)}) %copy-start.2) | copy-done | bytes 393240
  5.1 0.0 copy-start.3
  5.1 0.9 %copy-done.3 = bf16[256,384]{1,0:T(8,128)(2,1)S(1)} copy-done((bf16[256,384]{1,0:T(8,128)(2,1)S(1)}, bf16[256,384]{1,0:T(8,128)(2,1)}, u32[]{:S(2)}) %copy-start.3) | copy-done | bytes 196632
  6.0 0.0 copy-start.4
  6.0 0.9 %copy-done.4 = bf16[256,384]{1,0:T(8,128)(2,1)S(1)} copy-done((bf16[256,384]{1,0:T(8,128)(2,1)S(1)}, bf16[256,384]{1,0:T(8,128)(2,1)}, u32[]{:S(2)}) %copy-start.4) | copy-done | bytes 196632
  6.9 0.0 copy-start.5
  6.9 0.9 %copy-done.5 = bf16[256,384]{1,0:T(8,128)(2,1)S(1)} copy-done((bf16[256,384]{1,0:T(8,128)(2,1)S(1)}, bf16[256,384]{1,0:T(8,128)(2,1)}, u32[]{:S(2)}) %copy-start.5) | copy-done | bytes 196632
  7.8 0.0 copy-start.6
  7.8 0.7 copy-done.6
  8.5 0.0 copy-start.7
  8.5 0.7 copy-done.7
  9.3 0.0 copy-start.8
  9.3 0.7 copy-done.8
  10.0 0.0 copy-start.9
  10.0 0.7 copy-done.9
  10.6 0.7 copy-done.10
  11.3 58.5 %shard_map.118 = bf16[4,64,512]{2,1,0:T(8,128)(2,1)S(1)} custom-call(bf16[256,384]{1,0:T(8,128)(2,1)S(1)} %copy-done.3, bf16[256,384]{1,0:T(8,128)(2,1)S(1)} %copy-done.4, bf16[256,384]{1,0:T(8,128)(2,1)S(1)} %copy-done.5, s32[12]{0:T(128)S(1)} %copy-done.10, bf16[64,3072]{1,0:T(8,128)(2,1)S(1)} %copy-done.2, bf16[384,3072]{1,0:T(8,128)(2,1)S(1)} %copy-done, ...), custom_call_target="tpu_custom_call" | custom-call | tf_op jit(solution)/shard_map/pallas_call | solution.py:454
  69.8 0.7 %copy.15 = bf16[4,64,512]{2,1,0:T(8,128)(2,1)} copy(bf16[4,64,512]{2,1,0:T(8,128)(2,1)S(1)} %shard_map.118) | data formatting | bytes 524288
  (1 shorter events, 0.0 us)
Async XLA Ops:
  1.4 1.7 %copy-start = (bf16[384,3072]{1,0:T(8,128)(2,1)S(1)}, bf16[384,3072]{1,0:T(8,128)(2,1)}, u32[]{:S(2)}) copy-start(bf16[384,3072]{1,0:T(8,128)(2,1)} %w_hbm.1) | copy-start | bytes 7077892
  3.0 1.0 %copy-start.1 = (bf16[432,512]{1,0:T(8,128)(2,1)S(1)}, bf16[432,512]{1,0:T(8,128)(2,1)}, u32[]{:S(2)}) copy-start(bf16[432,512]{1,0:T(8,128)(2,1)} %dk_hbm.1) | copy-start | bytes 1327108
  4.1 1.0 %copy-start.2 = (bf16[64,3072]{1,0:T(8,128)(2,1)S(1)}, bf16[64,3072]{1,0:T(8,128)(2,1)}, u32[]{:S(2)}) copy-start(bf16[64,3072]{1,0:T(8,128)(2,1)} %res_hbm.1) | copy-start | bytes 1179652
  5.1 0.9 %copy-start.3 = (bf16[256,384]{1,0:T(8,128)(2,1)S(1)}, bf16[256,384]{1,0:T(8,128)(2,1)}, u32[]{:S(2)}) copy-start(bf16[256,384]{1,0:T(8,128)(2,1)} %q_hbm.1) | copy-start | bytes 589828
  6.0 0.9 %copy-start.4 = (bf16[256,384]{1,0:T(8,128)(2,1)S(1)}, bf16[256,384]{1,0:T(8,128)(2,1)}, u32[]{:S(2)}) copy-start(bf16[256,384]{1,0:T(8,128)(2,1)} %k_hbm.1) | copy-start | bytes 589828
  6.9 0.9 %copy-start.5 = (bf16[256,384]{1,0:T(8,128)(2,1)S(1)}, bf16[256,384]{1,0:T(8,128)(2,1)}, u32[]{:S(2)}) copy-start(bf16[256,384]{1,0:T(8,128)(2,1)} %v_hbm.1) | copy-start | bytes 589828
  7.8 0.7 %copy-start.6 = (f32[3072]{0:T(1024)S(1)}, f32[3072]{0:T(1024)}, u32[]{:S(2)}) copy-start(f32[3072]{0:T(1024)} %param.18) | copy-start | bytes 36868
  8.5 0.7 %copy-start.7 = (f32[3072]{0:T(1024)S(1)}, f32[3072]{0:T(1024)}, u32[]{:S(2)}) copy-start(f32[3072]{0:T(1024)} %param.19) | copy-start | bytes 36868
  9.3 0.7 %copy-start.8 = (f32[3072]{0:T(1024)S(1)}, f32[3072]{0:T(1024)}, u32[]{:S(2)}) copy-start(f32[3072]{0:T(1024)} %param.20) | copy-start | bytes 36868
  10.0 0.7 copy-start.9
  10.6 0.7 copy-start.10

commit v2 on v1

--- a/solution.py
+++ b/solution.py
@@ -159,9 +159,9 @@
 
 
 def fused_kernel(
-    q_hbm, k_hbm, v_hbm, lookback, res_hbm, w_hbm, gate_hbm, shift_hbm, scale_hbm, fw_hbm, dk_hbm, db_hbm,
+    q_hbm, k_hbm, v_hbm, look_hbm, res_hbm, w_hbm, gate_hbm, shift_hbm, scale_hbm, fw_hbm, dk_hbm, db_hbm,
     out_ref,
-    kz, kx, qv, wv, resv, gatev, shiftv, scalev, fwv, dkv, dbv,
+    lookback, kz, kx, qv, wv, resv, gatev, shiftv, scalev, fwv, dkv, dbv,
     top, total, acc, att, part, from_dec, to_y, from_y, hid, halo, wide, canvas,
     load_sem, kv_sem, zs, zr, xs, xr, ds, dr, ys, yr, hs, hr,
 ):
@@ -172,6 +172,20 @@
     n = f * 4 + hd * 2 + dc
     slab = q_hbm.shape[0]
     columns = w_hbm.shape[1] // CHUNKS
+
+    barrier = pltpu.get_barrier_semaphore()
+    greeted = jnp.int32(1)
+    pl.semaphore_signal(barrier, inc=1, device_id=(f, 1 - hd, dc), device_id_type=MESH)
+    for apart in (1, 3, 4, 5, 7, 8, 9):
+        for m in (n - apart, n + apart):
+            there = (m >= 0) & (m < 32)
+            greeted = greeted + jnp.where(there, 1, 0)
+
+            @pl.when(there)
+            def _():
+                pl.semaphore_signal(
+                    barrier, inc=1, device_id=(m // 4, (m % 4) // 2, m % 2), device_id_type=MESH
+                )
 
     kv_loads = []
     for h in range(HIGH):
@@ -185,7 +199,7 @@
         pltpu.make_async_copy(src, dst, load_sem.at[i])
         for i, (src, dst) in enumerate(
             (
-                (q_hbm, qv), (dk_hbm, dkv), (w_hbm, wv), (res_hbm, resv), (gate_hbm, gatev),
+                (q_hbm, qv), (dk_hbm, dkv), (look_hbm, lookback), (w_hbm, wv), (res_hbm, resv), (gate_hbm, gatev),
                 (shift_hbm, shiftv), (scale_hbm, scalev), (fw_hbm, fwv), (db_hbm, dbv),
             )
         )
@@ -217,10 +231,11 @@
     def across_comes(j):
         return z >= j + 1 - x
 
+    for c in kv_loads:
+        c.wait()
+    pl.semaphore_wait(barrier, greeted)
+
     for h in range(HIGH):
-        kv_loads[2 * h].wait()
-        kv_loads[2 * h + 1].wait()
-
         @pl.when(up_goes(0))
         def _():
             up(0, h).start()
@@ -237,7 +252,7 @@
         if distance == 0:
             newest = jnp.max(scores, axis=1, keepdims=True)
         else:
-            seen = lookback[(hd * 2 + dc) * HIGH + h] >= distance
+            seen = lookback[0, (hd * 2 + dc) * HIGH + h] >= distance
             scores = scores + jnp.where(seen, 0.0, -1e30)
             newest = jnp.maximum(top[h], jnp.max(scores, axis=1, keepdims=True))
         weights = jnp.exp(scores - newest).astype(jnp.bfloat16)
@@ -257,6 +272,7 @@
         attend(h, kz[0, h, 0], kz[0, h, 1], 0)
 
     loads[1].wait()
+    loads[2].wait()
     wide[...] = jnp.zeros_like(wide)
     for a in range(2):
         for b in range(2):
@@ -318,7 +334,7 @@
             device_id=(f, 1 - hd, dc), device_id_type=MESH,
         )
 
-    loads[2].wait()
+    loads[3].wait()
     for c in range(CHUNKS):
         share = jnp.dot(
             att[...], wv[:, c * columns : (c + 1) * columns], preferred_element_type=jnp.float32
@@ -331,7 +347,7 @@
             part[c, 1 - hd, dc].astype(jnp.float32) + from_dec[c, 1 - hd].astype(jnp.float32)
         ).astype(jnp.bfloat16)
         to_row(c).start()
-    for load in loads[3:]:
+    for load in loads[4:]:
         load.wait()
     summed = jnp.zeros((slab // 4, 1), jnp.float32)
     for c in range(CHUNKS):
@@ -346,11 +362,13 @@
     for c in range(CHUNKS):
         squares = squares + jnp.sum((hid[c] - center) ** 2, axis=1, keepdims=True)
     inverse = lax.rsqrt(squares / (CHUNKS * columns) + 1e-06)
-    patches = jnp.zeros((slab // 4, fwv.shape[1]), jnp.float32)
+    patches = jnp.zeros((slab // 4, fwv.shape[0]), jnp.float32)
     for c in range(CHUNKS):
         cols = slice(c * columns, (c + 1) * columns)
         normed = ((hid[c] - center) * inverse * (1.0 + scalev[:, cols]) + shiftv[:, cols]).astype(jnp.bfloat16)
-        patches = patches + jnp.dot(normed, fwv[cols, :], preferred_element_type=jnp.float32)
+        patches = patches + lax.dot_general(
+            normed, fwv[:, cols], (((1,), (1,)), ((), ())), preferred_element_type=jnp.float32
+        )
     halo[0, 1] = jnp.concatenate([patches, patches], axis=1).astype(jnp.bfloat16)
 
     def tile_to(back, side):
@@ -450,30 +468,31 @@
     outputs = decoder_kernel.shape[1]
     bf, f32 = jnp.bfloat16, jnp.float32
     vm, dma = pltpu.VMEM, pltpu.SemaphoreType.DMA
-    hbm = pl.BlockSpec(memory_space=pl.ANY)
+    hbm = pl.BlockSpec(memory_space=pltpu.HBM)
     return pl.pallas_call(
         fused_kernel,
         out_shape=jax.ShapeDtypeStruct((4, 2 * PW, outputs), bf),
-        in_specs=[hbm] * 3 + [pl.BlockSpec(memory_space=pltpu.SMEM)] + [hbm] * 8,
+        in_specs=[hbm] * 12,
         out_specs=pl.BlockSpec(memory_space=pltpu.VMEM),
         scratch_shapes=[
+            pltpu.SMEM((1, lookback.shape[0]), jnp.int32),
             vm((4, HIGH, 2, slab, DH), bf), vm((3, HIGH, 2, slab, DH), bf), vm((slab, width), bf),
             vm((width, model), bf), vm((quarter, model), bf),
             vm((1, model), f32), vm((1, model), f32), vm((1, model), f32),
-            vm(final_weight.shape, bf), vm(decoder_kernel.shape, bf), vm((1, outputs), f32),
+            vm(final_weight.shape[::-1], bf), vm(decoder_kernel.shape, bf), vm((1, outputs), f32),
             vm((HIGH, slab, 1), f32), vm((HIGH, slab, 1), f32), vm((HIGH, slab, DH), f32),
             vm((slab, width), bf), vm((CHUNKS, 2, 2, quarter, columns), bf),
             vm((CHUNKS, 2, quarter, columns), bf), vm((CHUNKS, quarter, columns), bf),
             vm((CHUNKS, quarter, columns), bf), vm((CHUNKS, quarter, columns), f32),
             vm((3, 3, quarter, 128), bf), vm((4, 768, outputs), bf), vm((outputs // 128, 256, 128), f32),
-            dma((9,)), dma((6,)), dma((3, HIGH)), dma((4, HIGH)), dma((3, HIGH)), dma((3, HIGH)),
+            dma((10,)), dma((6,)), dma((3, HIGH)), dma((4, HIGH)), dma((3, HIGH)), dma((3, HIGH)),
             dma((CHUNKS,)), dma((CHUNKS,)), dma((CHUNKS,)), dma((CHUNKS,)), dma((3, 3)), dma((3, 3)),
         ],
-        compiler_params=pltpu.CompilerParams(has_side_effects=True, vmem_limit_bytes=48 * 1024 * 1024),
+        compiler_params=pltpu.CompilerParams(collective_id=0, has_side_effects=True, vmem_limit_bytes=60 * 1024 * 1024),
     )(
-        queries, key_vectors, values, lookback, residual, out_weight,
+        queries, key_vectors, values, lookback.reshape(1, -1), residual, out_weight,
         branch_gate.reshape(1, -1), final_shift.reshape(1, -1), final_scale.reshape(1, -1),
-        final_weight, decoder_kernel, decoder_bias.reshape(1, -1),
+        final_weight.T, decoder_kernel, decoder_bias.reshape(1, -1),
     )
 
 

time: 71 us -> 56 us (0.79)
  local copies, waits for them, and re-layouts: 12 us -> 1.67 us
  Pallas kernels: 58.5 us -> 54.2 us
    unnamed x24 -> x1, local copies, waits for them, and re-layouts: 12 us -> 1.67 us
    pallas_call x1, Pallas kernels: 58.5 us -> 54.2 us  [fused(): pl.pallas_call(fused_kernel, out_shape=jax.ShapeDtypeStruct((4, 2 * PW, o...]
where the time goes in v2:
time: 56 us; the launch traced here: 55.9 us
  Pallas kernels  54.2 us (97%)
  local copies, waits for them, and re-layouts  1.67 us (3%)
    pallas_call x1, Pallas kernels, fused(): pl.pallas_call(fused_kernel, out_shape=jax.ShapeDtypeStruct((4, 2 * PW, o...  54.2 us
    unnamed x1, local copies, waits for them, and re-layouts  1.67 us

profile of v2, /device:TPU:23, one launch (start us, length us, event | category | flops | bytes accessed | tf_op | source)
XLA Modules:
  0.0 55.9 jit_solution(3904739066883341369)
XLA Ops:
  0.0 54.2 %shard_map.118 = bf16[4,64,512]{2,1,0:T(8,128)(2,1)} custom-call(bf16[256,384]{1,0:T(8,128)(2,1)} %q_hbm.1, bf16[256,384]{1,0:T(8,128)(2,1)} %k_hbm.1, bf16[256,384]{1,0:T(8,128)(2,1)} %v_hbm.1, s32[1,12]{1,0:T(1,128)} %bitcast.11, bf16[64,3072]{1,0:T(8,128)(2,1)} %res_hbm.1, bf16[384,3072]{1,0:T(8,128)(2,1)} %w_hbm.1, f32[1,3072]{1,0:T(1,128)} %bitcast.7, ...), custom_call_target="tpu_custom_call" | custom-call | tf_op jit(solution)/shard_map/pallas_call | solution.py:472
  54.2 1.7 %copy.14 = bf16[4,64,512]{2,1,0:T(8,128)(2,1)} copy(bf16[4,64,512]{2,1,0:T(8,128)(2,1)} %shard_map.118) | data formatting | bytes 524288

commit v3 on v2

--- a/solution.py
+++ b/solution.py
@@ -1,3 +1,5 @@
+import functools
+
 import jax
 import jax.numpy as jnp
 from jax import lax
@@ -161,9 +163,9 @@
 def fused_kernel(
     q_hbm, k_hbm, v_hbm, look_hbm, res_hbm, w_hbm, gate_hbm, shift_hbm, scale_hbm, fw_hbm, dk_hbm, db_hbm,
     out_ref,
-    lookback, kz, kx, qv, wv, resv, gatev, shiftv, scalev, fwv, dkv, dbv,
+    lookback, kz, kx, qv, asked, mixed_out, mixed_in, level_out, level_in, wv, resv, gatev, shiftv, scalev, fwv, dkv, dbv,
     top, total, acc, att, part, from_dec, to_y, from_y, hid, halo, wide, canvas,
-    load_sem, kv_sem, zs, zr, xs, xr, ds, dr, ys, yr, hs, hr,
+    load_sem, kv_sem, zs, zr, xs, xr, qs, qr, os, orr, ls, lr, ds, dr, ys, yr, hs, hr,
 ):
     f = lax.axis_index("blk")
     hd = lax.axis_index("head")
@@ -186,6 +188,12 @@
                 pl.semaphore_signal(
                     barrier, inc=1, device_id=(m // 4, (m % 4) // 2, m % 2), device_id_type=MESH
                 )
+
+    @pl.when((f == 2) | (f == 6))
+    def _():
+        pl.semaphore_signal(barrier, inc=1, device_id=(8 - f, hd, dc), device_id_type=MESH)
+
+    greeted = greeted + jnp.where((f == 2) | (f == 6), 1, 0)
 
     kv_loads = []
     for h in range(HIGH):
@@ -199,7 +207,8 @@
         pltpu.make_async_copy(src, dst, load_sem.at[i])
         for i, (src, dst) in enumerate(
             (
-                (q_hbm, qv), (dk_hbm, dkv), (look_hbm, lookback), (w_hbm, wv), (res_hbm, resv), (gate_hbm, gatev),
+                *[(q_hbm.at[:, pl.ds(h * DH, DH)], qv.at[h]) for h in range(HIGH)],
+                (dk_hbm, dkv), (look_hbm, lookback), (w_hbm, wv), (res_hbm, resv), (gate_hbm, gatev),
                 (shift_hbm, shiftv), (scale_hbm, scalev), (fw_hbm, fwv), (db_hbm, dbv),
             )
         )
@@ -207,72 +216,156 @@
     for c in kv_loads + loads:
         c.start()
 
-    def up(j, h):
+    def up(h):
         return pltpu.make_async_remote_copy(
-            src_ref=kz.at[j, h], dst_ref=kz.at[j + 1, h], send_sem=zs.at[j, h], recv_sem=zr.at[j + 1, h],
+            src_ref=kz.at[0, h], dst_ref=kz.at[1, h], send_sem=zs.at[h], recv_sem=zr.at[h],
             device_id=(f + 2, hd, dc), device_id_type=MESH,
         )
 
-    def across(j, h):
+    def own_across(h):
         return pltpu.make_async_remote_copy(
-            src_ref=kz.at[j + x, h], dst_ref=kx.at[j, h], send_sem=xs.at[j, h], recv_sem=xr.at[j, h],
+            src_ref=kz.at[0, h], dst_ref=kx.at[0, h], send_sem=xs.at[0, h], recv_sem=xr.at[0, h],
+            device_id=(f + 1, hd, dc), device_id_type=MESH,
+        )
+
+    def lower_across(h):
+        return pltpu.make_async_remote_copy(
+            src_ref=kz.at[1, h], dst_ref=kx.at[1 - x, h], send_sem=xs.at[1, h], recv_sem=xr.at[1 - x, h],
             device_id=(f + 1 - 2 * x, hd, dc), device_id_type=MESH,
         )
 
-    def up_goes(j):
-        return (z >= j) & (z < 3) & ((x == 1) | (j < 2))
-
-    def up_comes(j):
-        return (z >= j) & ((x == 1) | (j < 3))
-
-    def across_goes(j):
-        return z >= j + x
-
-    def across_comes(j):
-        return z >= j + 1 - x
+    def arrived(slot, h):
+        pltpu.make_async_remote_copy(
+            src_ref=kz.at[1, h], dst_ref=kx.at[slot, h], send_sem=xs.at[1, h], recv_sem=xr.at[slot, h],
+            device_id=(f + 1 - 2 * x, hd, dc), device_id_type=MESH,
+        ).wait_recv()
+
+    def ask(far, h):
+        return pltpu.make_async_remote_copy(
+            src_ref=qv.at[h], dst_ref=asked.at[far, h], send_sem=qs.at[far, h], recv_sem=qr.at[far, h],
+            device_id=(f - 2 - 2 * far, hd, dc), device_id_type=MESH,
+        )
+
+    def answer(far, h):
+        to = (f + 2 + 2 * far, hd, dc)
+        return (
+            pltpu.make_async_remote_copy(
+                src_ref=mixed_out.at[far, h], dst_ref=mixed_in.at[far, h],
+                send_sem=os.at[far, h], recv_sem=orr.at[far, h], device_id=to, device_id_type=MESH,
+            ),
+            pltpu.make_async_remote_copy(
+                src_ref=level_out.at[far, h], dst_ref=level_in.at[far, h],
+                send_sem=ls.at[far, h], recv_sem=lr.at[far, h], device_id=to, device_id_type=MESH,
+            ),
+        )
+
+    asks = (z >= 2, f == 6)
+    helps = ((z >= 1) & (z <= 2), f == 2)
 
     for c in kv_loads:
         c.wait()
+    for h in range(HIGH):
+        loads[h].wait()
     pl.semaphore_wait(barrier, greeted)
 
     for h in range(HIGH):
-        @pl.when(up_goes(0))
-        def _():
-            up(0, h).start()
-
-        @pl.when(x == 0)
-        def _():
-            across(0, h).start()
-
-    def attend(h, key, value, distance):
-        query = qv[:, h * DH : (h + 1) * DH]
+
+        @pl.when(z < 3)
+        def _():
+            up(h).start()
+
+        for far in range(2):
+
+            @pl.when(asks[far])
+            def _():
+                ask(far, h).start()
+
+        @pl.when((x == 0) & ((z == 0) | (h == 0)))
+        def _():
+            own_across(h).start()
+
+    def scored(query, key, h, distance):
         scores = lax.dot_general(
             query, key, (((1,), (1,)), ((), ())), preferred_element_type=jnp.float32
         ) * DH ** (-0.5)
-        if distance == 0:
-            newest = jnp.max(scores, axis=1, keepdims=True)
-        else:
-            seen = lookback[0, (hd * 2 + dc) * HIGH + h] >= distance
-            scores = scores + jnp.where(seen, 0.0, -1e30)
-            newest = jnp.maximum(top[h], jnp.max(scores, axis=1, keepdims=True))
+        if isinstance(distance, int) and distance == 0:
+            return scores
+        seen = lookback[0, (hd * 2 + dc) * HIGH + h] >= distance
+        return scores + jnp.where(seen, 0.0, -1e30)
+
+    def weighed(scores, newest, value):
         weights = jnp.exp(scores - newest).astype(jnp.bfloat16)
         added = jnp.sum(weights.astype(jnp.float32), axis=1, keepdims=True)
-        mixed = jnp.dot(weights, value, preferred_element_type=jnp.float32)
-        if distance == 0:
-            total[h] = added
-            acc[h] = mixed
+        return added, jnp.dot(weights, value, preferred_element_type=jnp.float32)
+
+    def attend(h, key, value, distance):
+        scores = scored(qv[h], key, h, distance)
+        newest = jnp.max(scores, axis=1, keepdims=True)
+        if isinstance(distance, int) and distance == 0:
+            total[h], acc[h] = weighed(scores, newest, value)
         else:
+            newest = jnp.maximum(top[h], newest)
+            added, mixed = weighed(scores, newest, value)
             shrink = jnp.exp(top[h] - newest)
             total[h] = total[h] * shrink + added
             acc[h] = acc[h] * shrink + mixed
         top[h] = newest
 
-    loads[0].wait()
+    def help_with(far, h, blocks):
+        @pl.when(helps[far])
+        def _():
+            ask(far, h).wait_recv()
+            query = asked[far, h]
+            scores = [scored(query, key, h, distance) for key, _, distance in blocks]
+            newest = functools.reduce(
+                jnp.maximum, [jnp.max(each, axis=1, keepdims=True) for each in scores]
+            )
+            parts = [weighed(each, newest, block[1]) for each, block in zip(scores, blocks)]
+            added = functools.reduce(jnp.add, [part[0] for part in parts])
+            mixed = functools.reduce(jnp.add, [part[1] for part in parts])
+            mixed_out[far, h] = (mixed / added).astype(jnp.bfloat16)
+            level = jnp.broadcast_to(newest + jnp.log(added), (slab, 128))
+            level_out[far, h] = level.T[:8]
+            for copy in answer(far, h):
+                copy.start()
+
+    loads[HIGH].wait()
+    loads[HIGH + 1].wait()
     for h in range(HIGH):
         attend(h, kz[0, h, 0], kz[0, h, 1], 0)
 
-    loads[1].wait()
-    loads[2].wait()
+    for h in range(HIGH):
+
+        @pl.when(z >= 1)
+        def _():
+            up(h).wait_recv()
+            lower_across(h).start()
+            if h == HIGH - 1:
+
+                @pl.when(x == 0)
+                def _():
+                    for late in range(1, HIGH):
+                        own_across(late).start()
+
+            attend(h, kz[1, h, 0], kz[1, h, 1], 2)
+
+    for h in range(HIGH):
+
+        @pl.when(z >= 1)
+        def _():
+            arrived(x, h)
+            lower = (kx[x, h, 0], kx[x, h, 1], 3 + 2 * x)
+            help_with(0, h, (lower, (kz[1, h, 0], kz[1, h, 1], 4)))
+            help_with(1, h, ((lower[0], lower[1], 5),))
+            attend(h, kx[x, h, 0], kx[x, h, 1], 1 + 2 * x)
+
+    for h in range(HIGH):
+
+        @pl.when(x == 1)
+        def _():
+            arrived(0, h)
+            attend(h, kx[0, h, 0], kx[0, h, 1], 1)
+
     wide[...] = jnp.zeros_like(wide)
     for a in range(2):
         for b in range(2):
@@ -285,39 +378,20 @@
                         tap = (t * 3 + i) * 3 + j
                         wide[a * 2 + b, row : row + LC, :] = dkv[tap * LC : (tap + 1) * LC, :]
 
-    def z_part(j, h):
-        @pl.when(up_comes(j))
-        def _():
-            up(j - 1, h).wait_recv()
-            if j <= 2:
-
-                @pl.when(up_goes(j))
-                def _():
-                    up(j, h).start()
-
-                @pl.when(x == 0)
-                def _():
-                    across(j, h).start()
-
-            @pl.when(x == 1)
+
+    for far in range(2):
+        for h in range(HIGH):
+
+            @pl.when(asks[far])
             def _():
-                across(j - 1, h).start()
-
-            if j <= 2:
-                attend(h, kz[j, h, 0], kz[j, h, 1], 2 * j)
-
-    def x_part(j, h):
-        @pl.when(across_comes(j))
-        def _():
-            across(j, h).wait_recv()
-            attend(h, kx[j, h, 0], kx[j, h, 1], 2 * j + 1)
-
-    order = [(j, h) for j in range(1, 4) for h in range(HIGH)]
-    for place, (j, h) in enumerate(order):
-        z_part(j, h)
-        if place:
-            x_part(order[place - 1][0] - 1, order[place - 1][1])
-    x_part(order[-1][0] - 1, order[-1][1])
+                for copy in answer(far, h):
+                    copy.wait_recv()
+                level = jnp.broadcast_to(level_in[far, h][:1], (128, slab)).T[:, :1]
+                newest = jnp.maximum(top[h], level)
+                shrink, grow = jnp.exp(top[h] - newest), jnp.exp(level - newest)
+                total[h] = total[h] * shrink + grow
+                acc[h] = acc[h] * shrink + mixed_in[far, h].astype(jnp.float32) * grow
+                top[h] = newest
 
     for h in range(HIGH):
         att[:, h * DH : (h + 1) * DH] = (acc[h] / total[h]).astype(jnp.bfloat16)
@@ -334,7 +408,7 @@
             device_id=(f, 1 - hd, dc), device_id_type=MESH,
         )
 
-    loads[3].wait()
+    loads[HIGH + 2].wait()
     for c in range(CHUNKS):
         share = jnp.dot(
             att[...], wv[:, c * columns : (c + 1) * columns], preferred_element_type=jnp.float32
@@ -347,7 +421,7 @@
             part[c, 1 - hd, dc].astype(jnp.float32) + from_dec[c, 1 - hd].astype(jnp.float32)
         ).astype(jnp.bfloat16)
         to_row(c).start()
-    for load in loads[4:]:
+    for load in loads[HIGH + 3 :]:
         load.wait()
     summed = jnp.zeros((slab // 4, 1), jnp.float32)
     for c in range(CHUNKS):
@@ -436,16 +510,30 @@
         for g in range(canvas.shape[0]):
             out_ref[y, :, g * 128 : (g + 1) * 128] = canvas[g, y * 2 * PW : (y + 1) * 2 * PW, :].astype(jnp.bfloat16)
 
-    for j in range(3):
-        for h in range(HIGH):
-
-            @pl.when(up_goes(j))
+    for h in range(HIGH):
+
+        @pl.when(z < 3)
+        def _():
+            up(h).wait_send()
+
+        @pl.when(z >= 1)
+        def _():
+            lower_across(h).wait_send()
+
+        @pl.when(x == 0)
+        def _():
+            own_across(h).wait_send()
+
+        for far in range(2):
+
+            @pl.when(asks[far])
             def _():
-                up(j, h).wait_send()
-
-            @pl.when(across_goes(j))
+                ask(far, h).wait_send()
+
+            @pl.when(helps[far])
             def _():
-                across(j, h).wait_send()
+                for copy in answer(far, h):
+                    copy.wait_send()
 
     for c in range(CHUNKS):
         to_core(c).wait_send()
@@ -476,7 +564,8 @@
         out_specs=pl.BlockSpec(memory_space=pltpu.VMEM),
         scratch_shapes=[
             pltpu.SMEM((1, lookback.shape[0]), jnp.int32),
-            vm((4, HIGH, 2, slab, DH), bf), vm((3, HIGH, 2, slab, DH), bf), vm((slab, width), bf),
+            vm((2, HIGH, 2, slab, DH), bf), vm((2, HIGH, 2, slab, DH), bf), vm((HIGH, slab, DH), bf),
+            *[vm((2, HIGH, slab, DH), bf)] * 3, *[vm((2, HIGH, 8, slab), f32)] * 2,
             vm((width, model), bf), vm((quarter, model), bf),
             vm((1, model), f32), vm((1, model), f32), vm((1, model), f32),
             vm(final_weight.shape[::-1], bf), vm(decoder_kernel.shape, bf), vm((1, outputs), f32),
@@ -485,7 +574,8 @@
             vm((CHUNKS, 2, quarter, columns), bf), vm((CHUNKS, quarter, columns), bf),
             vm((CHUNKS, quarter, columns), bf), vm((CHUNKS, quarter, columns), f32),
             vm((3, 3, quarter, 128), bf), vm((4, 768, outputs), bf), vm((outputs // 128, 256, 128), f32),
-            dma((10,)), dma((6,)), dma((3, HIGH)), dma((4, HIGH)), dma((3, HIGH)), dma((3, HIGH)),
+            dma((HIGH + 9,)), dma((6,)), dma((HIGH,)), dma((HIGH,)), dma((2, HIGH)), dma((2, HIGH)),
+            *[dma((2, HIGH))] * 6,
             dma((CHUNKS,)), dma((CHUNKS,)), dma((CHUNKS,)), dma((CHUNKS,)), dma((3, 3)), dma((3, 3)),
         ],
         compiler_params=pltpu.CompilerParams(collective_id=0, has_side_effects=True, vmem_limit_bytes=60 * 1024 * 1024),

time: 56 us -> 45.5 us (0.81)
  Pallas kernels: 54.2 us -> 43.6 us
    pallas_call x1, Pallas kernels: 54.2 us -> 43.6 us  [fused(): pl.pallas_call(fused_kernel, out_shape=jax.ShapeDtypeStruct((4, 2 * PW, o...]
where the time goes in v3:
time: 45.5 us; the launch traced here: 45.3 us
  Pallas kernels  43.6 us (96%)
  local copies, waits for them, and re-layouts  1.67 us (4%)
    pallas_call x1, Pallas kernels, fused(): pl.pallas_call(fused_kernel, out_shape=jax.ShapeDtypeStruct((4, 2 * PW, o...  43.6 us
    unnamed x1, local copies, waits for them, and re-layouts  1.67 us

profile of v3, /device:TPU:23, one launch (start us, length us, event | category | flops | bytes accessed | tf_op | source)
XLA Modules:
  0.0 45.3 jit_solution(16340949422666517737)
XLA Ops:
  0.0 43.6 %shard_map.118 = bf16[4,64,512]{2,1,0:T(8,128)(2,1)} custom-call(bf16[256,384]{1,0:T(8,128)(2,1)} %q_hbm.1, bf16[256,384]{1,0:T(8,128)(2,1)} %k_hbm.1, bf16[256,384]{1,0:T(8,128)(2,1)} %v_hbm.1, s32[1,12]{1,0:T(1,128)} %bitcast.11, bf16[64,3072]{1,0:T(8,128)(2,1)} %res_hbm.1, bf16[384,3072]{1,0:T(8,128)(2,1)} %w_hbm.1, f32[1,3072]{1,0:T(1,128)} %bitcast.7, ...), custom_call_target="tpu_custom_call" | custom-call | tf_op jit(solution)/shard_map/pallas_call | solution.py:560
  43.6 1.7 %copy.14 = bf16[4,64,512]{2,1,0:T(8,128)(2,1)} copy(bf16[4,64,512]{2,1,0:T(8,128)(2,1)} %shard_map.118) | data formatting | bytes 524288

commit v4 on v3

--- a/solution.py
+++ b/solution.py
@@ -156,7 +156,9 @@
 
 
 HIGH = 3
-CHUNKS = 4
+CHUNKS = 6
+STEPS = (2, 4, 1)
+SIDE = (1, 2)
 MESH = pl.DeviceIdType.MESH
 
 
@@ -243,11 +245,11 @@
     def ask(far, h):
         return pltpu.make_async_remote_copy(
             src_ref=qv.at[h], dst_ref=asked.at[far, h], send_sem=qs.at[far, h], recv_sem=qr.at[far, h],
-            device_id=(f - 2 - 2 * far, hd, dc), device_id_type=MESH,
+            device_id=(f - STEPS[far], hd, dc), device_id_type=MESH,
         )
 
     def answer(far, h):
-        to = (f + 2 + 2 * far, hd, dc)
+        to = (f + STEPS[far], hd, dc)
         return (
             pltpu.make_async_remote_copy(
                 src_ref=mixed_out.at[far, h], dst_ref=mixed_in.at[far, h],
@@ -259,8 +261,12 @@
             ),
         )
 
-    asks = (z >= 2, f == 6)
-    helps = ((z >= 1) & (z <= 2), f == 2)
+    asks = (z >= 2, f == 6, x == 1)
+    helps = ((z >= 1) & (z <= 2), f == 2, x == 0)
+
+    def kinds(h):
+        return (0, 1, 2) if h in SIDE else (0, 1)
+
 
     for c in kv_loads:
         c.wait()
@@ -274,15 +280,17 @@
         def _():
             up(h).start()
 
-        for far in range(2):
+        for far in kinds(h):
 
             @pl.when(asks[far])
             def _():
                 ask(far, h).start()
 
-        @pl.when((x == 0) & ((z == 0) | (h == 0)))
-        def _():
-            own_across(h).start()
+        if h not in SIDE:
+
+            @pl.when(x == 0)
+            def _():
+                own_across(h).start()
 
     def scored(query, key, h, distance):
         scores = lax.dot_general(
@@ -340,31 +348,10 @@
         def _():
             up(h).wait_recv()
             lower_across(h).start()
-            if h == HIGH - 1:
-
-                @pl.when(x == 0)
-                def _():
-                    for late in range(1, HIGH):
-                        own_across(late).start()
-
             attend(h, kz[1, h, 0], kz[1, h, 1], 2)
 
-    for h in range(HIGH):
-
-        @pl.when(z >= 1)
-        def _():
-            arrived(x, h)
-            lower = (kx[x, h, 0], kx[x, h, 1], 3 + 2 * x)
-            help_with(0, h, (lower, (kz[1, h, 0], kz[1, h, 1], 4)))
-            help_with(1, h, ((lower[0], lower[1], 5),))
-            attend(h, kx[x, h, 0], kx[x, h, 1], 1 + 2 * x)
-
-    for h in range(HIGH):
-
-        @pl.when(x == 1)
-        def _():
-            arrived(0, h)
-            attend(h, kx[0, h, 0], kx[0, h, 1], 1)
+    for h in SIDE:
+        help_with(2, h, ((kz[0, h, 0], kz[0, h, 1], 1),))
 
     wide[...] = jnp.zeros_like(wide)
     for a in range(2):
@@ -378,9 +365,27 @@
                         tap = (t * 3 + i) * 3 + j
                         wide[a * 2 + b, row : row + LC, :] = dkv[tap * LC : (tap + 1) * LC, :]
 
-
-    for far in range(2):
-        for h in range(HIGH):
+    for h in range(HIGH):
+
+        @pl.when(z >= 1)
+        def _():
+            arrived(x, h)
+            lower = (kx[x, h, 0], kx[x, h, 1], 3 + 2 * x)
+            help_with(0, h, (lower, (kz[1, h, 0], kz[1, h, 1], 4)))
+            help_with(1, h, ((lower[0], lower[1], 5),))
+            attend(h, kx[x, h, 0], kx[x, h, 1], 1 + 2 * x)
+
+    for h in range(HIGH):
+        if h in SIDE:
+            continue
+
+        @pl.when(x == 1)
+        def _():
+            arrived(0, h)
+            attend(h, kx[0, h, 0], kx[0, h, 1], 1)
+
+    for far in (2, 1, 0):
+        for h in SIDE if far == 2 else range(HIGH):
 
             @pl.when(asks[far])
             def _():
@@ -394,11 +399,12 @@
                 top[h] = newest
 
     for h in range(HIGH):
-        att[:, h * DH : (h + 1) * DH] = (acc[h] / total[h]).astype(jnp.bfloat16)
-
-    def to_core(c):
+        att[:, :, h * DH : (h + 1) * DH] = (acc[h] / total[h]).astype(jnp.bfloat16).reshape(2, slab // 2, DH)
+
+    def to_core(half, c):
         return pltpu.make_async_remote_copy(
-            src_ref=part.at[c, :, 1 - dc], dst_ref=from_dec.at[c], send_sem=ds.at[c], recv_sem=dr.at[c],
+            src_ref=part.at[c, half, 1 - dc], dst_ref=from_dec.at[c, half],
+            send_sem=ds.at[half, c], recv_sem=dr.at[half, c],
             device_id=(f, hd, 1 - dc), device_id_type=MESH,
         )
 
@@ -409,26 +415,39 @@
         )
 
     loads[HIGH + 2].wait()
+    def share(half, c):
+        got = jnp.dot(
+            att[half], wv[:, c * columns : (c + 1) * columns], preferred_element_type=jnp.float32
+        ).astype(jnp.bfloat16)
+        part[c, half] = got.reshape(2, slab // 4, columns)
+        to_core(half, c).start()
+
+    def both_cores(half, c):
+        to_core(half, c).wait_recv()
+        return part[c, half, dc].astype(jnp.float32) + from_dec[c, half].astype(jnp.float32)
+
+    def pass_on(c):
+        to_y[c] = both_cores(1 - hd, c).astype(jnp.bfloat16)
+        to_row(c).start()
+
     for c in range(CHUNKS):
-        share = jnp.dot(
-            att[...], wv[:, c * columns : (c + 1) * columns], preferred_element_type=jnp.float32
-        ).astype(jnp.bfloat16)
-        part[c] = share.reshape(2, 2, slab // 4, columns)
-        to_core(c).start()
+        share(1 - hd, c)
+        if c >= 2:
+            pass_on(c - 2)
+    pass_on(CHUNKS - 2)
+    pass_on(CHUNKS - 1)
     for c in range(CHUNKS):
-        to_core(c).wait_recv()
-        to_y[c] = (
-            part[c, 1 - hd, dc].astype(jnp.float32) + from_dec[c, 1 - hd].astype(jnp.float32)
-        ).astype(jnp.bfloat16)
-        to_row(c).start()
+        share(hd, c)
     for load in loads[HIGH + 3 :]:
         load.wait()
+    for c in range(CHUNKS):
+        cols = slice(c * columns, (c + 1) * columns)
+        hid[c] = resv[:, cols].astype(jnp.float32) + gatev[:, cols] * both_cores(hd, c)
     summed = jnp.zeros((slab // 4, 1), jnp.float32)
     for c in range(CHUNKS):
         cols = slice(c * columns, (c + 1) * columns)
-        mine = part[c, hd, dc].astype(jnp.float32) + from_dec[c, hd].astype(jnp.float32)
         to_row(c).wait_recv()
-        hidden = resv[:, cols].astype(jnp.float32) + gatev[:, cols] * (mine + from_y[c].astype(jnp.float32))
+        hidden = hid[c] + gatev[:, cols] * from_y[c].astype(jnp.float32)
         hid[c] = hidden
         summed = summed + jnp.sum(hidden, axis=1, keepdims=True)
     center = summed / (CHUNKS * columns)
@@ -520,11 +539,13 @@
         def _():
             lower_across(h).wait_send()
 
-        @pl.when(x == 0)
-        def _():
-            own_across(h).wait_send()
-
-        for far in range(2):
+        if h not in SIDE:
+
+            @pl.when(x == 0)
+            def _():
+                own_across(h).wait_send()
+
+        for far in kinds(h):
 
             @pl.when(asks[far])
             def _():
@@ -536,7 +557,8 @@
                     copy.wait_send()
 
     for c in range(CHUNKS):
-        to_core(c).wait_send()
+        to_core(hd, c).wait_send()
+        to_core(1 - hd, c).wait_send()
         to_row(c).wait_send()
     for back, side in reach:
         copy, goes = tile_to(back, side)
@@ -559,24 +581,24 @@
     hbm = pl.BlockSpec(memory_space=pltpu.HBM)
     return pl.pallas_call(
         fused_kernel,
-        out_shape=jax.ShapeDtypeStruct((4, 2 * PW, outputs), bf),
+        out_shape=pltpu.VMEM((4, 2 * PW, outputs), bf),
         in_specs=[hbm] * 12,
         out_specs=pl.BlockSpec(memory_space=pltpu.VMEM),
         scratch_shapes=[
             pltpu.SMEM((1, lookback.shape[0]), jnp.int32),
             vm((2, HIGH, 2, slab, DH), bf), vm((2, HIGH, 2, slab, DH), bf), vm((HIGH, slab, DH), bf),
-            *[vm((2, HIGH, slab, DH), bf)] * 3, *[vm((2, HIGH, 8, slab), f32)] * 2,
+            *[vm((3, HIGH, slab, DH), bf)] * 3, *[vm((3, HIGH, 8, slab), f32)] * 2,
             vm((width, model), bf), vm((quarter, model), bf),
             vm((1, model), f32), vm((1, model), f32), vm((1, model), f32),
             vm(final_weight.shape[::-1], bf), vm(decoder_kernel.shape, bf), vm((1, outputs), f32),
             vm((HIGH, slab, 1), f32), vm((HIGH, slab, 1), f32), vm((HIGH, slab, DH), f32),
-            vm((slab, width), bf), vm((CHUNKS, 2, 2, quarter, columns), bf),
+            vm((2, slab // 2, width), bf), vm((CHUNKS, 2, 2, quarter, columns), bf),
             vm((CHUNKS, 2, quarter, columns), bf), vm((CHUNKS, quarter, columns), bf),
             vm((CHUNKS, quarter, columns), bf), vm((CHUNKS, quarter, columns), f32),
             vm((3, 3, quarter, 128), bf), vm((4, 768, outputs), bf), vm((outputs // 128, 256, 128), f32),
             dma((HIGH + 9,)), dma((6,)), dma((HIGH,)), dma((HIGH,)), dma((2, HIGH)), dma((2, HIGH)),
-            *[dma((2, HIGH))] * 6,
-            dma((CHUNKS,)), dma((CHUNKS,)), dma((CHUNKS,)), dma((CHUNKS,)), dma((3, 3)), dma((3, 3)),
+            *[dma((3, HIGH))] * 6,
+            dma((2, CHUNKS)), dma((2, CHUNKS)), dma((CHUNKS,)), dma((CHUNKS,)), dma((3, 3)), dma((3, 3)),
         ],
         compiler_params=pltpu.CompilerParams(collective_id=0, has_side_effects=True, vmem_limit_bytes=60 * 1024 * 1024),
     )(

time: 45.5 us -> 45.8 us (level)
  Pallas kernels: 43.6 us -> 44.9 us
  local copies, waits for them, and re-layouts: 1.67 us -> 0.71 us
    pallas_call x1, Pallas kernels: 43.6 us -> 44.9 us  [fused(): pl.pallas_call(fused_kernel, out_shape=pltpu.VMEM((4, 2 * PW, outputs), b...]
    unnamed x1, local copies, waits for them, and re-layouts: 1.67 us -> 0.71 us
where the time goes in v4:
time: 45.8 us; the launch traced here: 45.6 us
  Pallas kernels  44.9 us (98%)
  local copies, waits for them, and re-layouts  0.71 us (2%)
    pallas_call x1, Pallas kernels, fused(): pl.pallas_call(fused_kernel, out_shape=pltpu.VMEM((4, 2 * PW, outputs), b...  44.9 us

profile of v4, /device:TPU:23, one launch (start us, length us, event | category | flops | bytes accessed | tf_op | source)
XLA Modules:
  0.0 45.6 jit_solution(15726783781574132265)
XLA Ops:
  0.0 44.9 %shard_map.118 = bf16[4,64,512]{2,1,0:T(8,128)(2,1)S(1)} custom-call(bf16[256,384]{1,0:T(8,128)(2,1)} %q_hbm.1, bf16[256,384]{1,0:T(8,128)(2,1)} %k_hbm.1, bf16[256,384]{1,0:T(8,128)(2,1)} %v_hbm.1, s32[1,12]{1,0:T(1,128)} %bitcast.11, bf16[64,3072]{1,0:T(8,128)(2,1)} %res_hbm.1, bf16[384,3072]{1,0:T(8,128)(2,1)} %w_hbm.1, f32[1,3072]{1,0:T(1,128)} %bitcast.7, ...), custom_call_target="tpu_custom_call" | custom-call | tf_op jit(solution)/shard_map/pallas_call | solution.py:582
  44.9 0.7 %copy.14 = bf16[4,64,512]{2,1,0:T(8,128)(2,1)} copy(bf16[4,64,512]{2,1,0:T(8,128)(2,1)S(1)} %shard_map.118) | data formatting | bytes 524288

commit v5 on v4

--- a/solution.py
+++ b/solution.py
@@ -159,6 +159,7 @@
 CHUNKS = 6
 STEPS = (2, 4, 1)
 SIDE = (1, 2)
+LOG2_E = 1.4426950408889634
 MESH = pl.DeviceIdType.MESH
 
 
@@ -292,48 +293,53 @@
             def _():
                 own_across(h).start()
 
-    def scored(query, key, h, distance):
-        scores = lax.dot_general(
-            query, key, (((1,), (1,)), ((), ())), preferred_element_type=jnp.float32
-        ) * DH ** (-0.5)
+    def scored(query, key):
+        return lax.dot_general(
+            key, query, (((1,), (1,)), ((), ())), preferred_element_type=jnp.float32
+        ) * (DH ** (-0.5) * LOG2_E)
+
+    def visible(h, distance):
+        return lookback[0, (hd * 2 + dc) * HIGH + h] >= distance
+
+    def weighed(scores, shift, value):
+        weights = jnp.exp2(scores + shift)
+        mixed = lax.dot_general(
+            value, weights.astype(jnp.bfloat16), (((0,), (0,)), ((), ())), preferred_element_type=jnp.float32
+        )
+        return jnp.sum(weights, axis=0, keepdims=True), mixed
+
+    def attend(h, key, value, distance):
+        scores = scored(qv[h], key)
+        highest = jnp.max(scores, axis=0, keepdims=True)
         if isinstance(distance, int) and distance == 0:
-            return scores
-        seen = lookback[0, (hd * 2 + dc) * HIGH + h] >= distance
-        return scores + jnp.where(seen, 0.0, -1e30)
-
-    def weighed(scores, newest, value):
-        weights = jnp.exp(scores - newest).astype(jnp.bfloat16)
-        added = jnp.sum(weights.astype(jnp.float32), axis=1, keepdims=True)
-        return added, jnp.dot(weights, value, preferred_element_type=jnp.float32)
-
-    def attend(h, key, value, distance):
-        scores = scored(qv[h], key, h, distance)
-        newest = jnp.max(scores, axis=1, keepdims=True)
-        if isinstance(distance, int) and distance == 0:
-            total[h], acc[h] = weighed(scores, newest, value)
+            total[h], acc[h] = weighed(scores, -highest, value)
+            top[h] = highest
         else:
-            newest = jnp.maximum(top[h], newest)
-            added, mixed = weighed(scores, newest, value)
-            shrink = jnp.exp(top[h] - newest)
+            seen = visible(h, distance)
+            newest = jnp.maximum(top[h], jnp.where(seen, highest, -1e30))
+            added, mixed = weighed(scores, jnp.where(seen, -newest, -1e30), value)
+            shrink = jnp.exp2(top[h] - newest)
             total[h] = total[h] * shrink + added
             acc[h] = acc[h] * shrink + mixed
-        top[h] = newest
+            top[h] = newest
 
     def help_with(far, h, blocks):
         @pl.when(helps[far])
         def _():
             ask(far, h).wait_recv()
             query = asked[far, h]
-            scores = [scored(query, key, h, distance) for key, _, distance in blocks]
-            newest = functools.reduce(
-                jnp.maximum, [jnp.max(each, axis=1, keepdims=True) for each in scores]
-            )
-            parts = [weighed(each, newest, block[1]) for each, block in zip(scores, blocks)]
-            added = functools.reduce(jnp.add, [part[0] for part in parts])
-            mixed = functools.reduce(jnp.add, [part[1] for part in parts])
+            newest, scores = jnp.full((1, slab), -1e30, jnp.float32), []
+            for key, _, distance in blocks:
+                scores.append(scored(query, key))
+                highest = jnp.max(scores[-1], axis=0, keepdims=True)
+                newest = jnp.maximum(newest, jnp.where(visible(h, distance), highest, -1e30))
+            added, mixed = 0.0, 0.0
+            for each, (_, value, distance) in zip(scores, blocks):
+                part_of = weighed(each, jnp.where(visible(h, distance), -newest, -1e30), value)
+                added, mixed = added + part_of[0], mixed + part_of[1]
+            added = jnp.where(added > 0.0, added, 1.0)
             mixed_out[far, h] = (mixed / added).astype(jnp.bfloat16)
-            level = jnp.broadcast_to(newest + jnp.log(added), (slab, 128))
-            level_out[far, h] = level.T[:8]
+            level_out[far, h] = jnp.broadcast_to(newest + jnp.log2(added), (8, slab))
             for copy in answer(far, h):
                 copy.start()
 
@@ -391,15 +397,15 @@
             def _():
                 for copy in answer(far, h):
                     copy.wait_recv()
-                level = jnp.broadcast_to(level_in[far, h][:1], (128, slab)).T[:, :1]
+                level = level_in[far, h][:1]
                 newest = jnp.maximum(top[h], level)
-                shrink, grow = jnp.exp(top[h] - newest), jnp.exp(level - newest)
+                shrink, grow = jnp.exp2(top[h] - newest), jnp.exp2(level - newest)
                 total[h] = total[h] * shrink + grow
                 acc[h] = acc[h] * shrink + mixed_in[far, h].astype(jnp.float32) * grow
                 top[h] = newest
 
     for h in range(HIGH):
-        att[:, :, h * DH : (h + 1) * DH] = (acc[h] / total[h]).astype(jnp.bfloat16).reshape(2, slab // 2, DH)
+        att[:, :, h * DH : (h + 1) * DH] = (acc[h] / total[h]).T.astype(jnp.bfloat16).reshape(2, slab // 2, DH)
 
     def to_core(half, c):
         return pltpu.make_async_remote_copy(
@@ -587,11 +593,11 @@
         scratch_shapes=[
             pltpu.SMEM((1, lookback.shape[0]), jnp.int32),
             vm((2, HIGH, 2, slab, DH), bf), vm((2, HIGH, 2, slab, DH), bf), vm((HIGH, slab, DH), bf),
-            *[vm((3, HIGH, slab, DH), bf)] * 3, *[vm((3, HIGH, 8, slab), f32)] * 2,
+            vm((3, HIGH, slab, DH), bf), *[vm((3, HIGH, DH, slab), bf)] * 2, *[vm((3, HIGH, 8, slab), f32)] * 2,
             vm((width, model), bf), vm((quarter, model), bf),
             vm((1, model), f32), vm((1, model), f32), vm((1, model), f32),
             vm(final_weight.shape[::-1], bf), vm(decoder_kernel.shape, bf), vm((1, outputs), f32),
-            vm((HIGH, slab, 1), f32), vm((HIGH, slab, 1), f32), vm((HIGH, slab, DH), f32),
+            vm((HIGH, 1, slab), f32), vm((HIGH, 1, slab), f32), vm((HIGH, DH, slab), f32),
             vm((2, slab // 2, width), bf), vm((CHUNKS, 2, 2, quarter, columns), bf),
             vm((CHUNKS, 2, quarter, columns), bf), vm((CHUNKS, quarter, columns), bf),
             vm((CHUNKS, quarter, columns), bf), vm((CHUNKS, quarter, columns), f32),

time: 45.8 us -> 45 us (0.983)
  Pallas kernels: 44.9 us -> 44.1 us
    pallas_call x1, Pallas kernels: 44.9 us -> 44.1 us  [fused(): pl.pallas_call(fused_kernel, out_shape=pltpu.VMEM((4, 2 * PW, outputs), b...]
where the time goes in v5:
time: 45 us; the launch traced here: 44.8 us
  Pallas kernels  44.1 us (98%)
  local copies, waits for them, and re-layouts  0.71 us (2%)
    pallas_call x1, Pallas kernels, fused(): pl.pallas_call(fused_kernel, out_shape=pltpu.VMEM((4, 2 * PW, outputs), b...  44.1 us

profile of v5, /device:TPU:23, one launch (start us, length us, event | category | flops | bytes accessed | tf_op | source)
XLA Modules:
  0.0 44.8 jit_solution(4319068232995339103)
XLA Ops:
  0.0 44.1 %shard_map.118 = bf16[4,64,512]{2,1,0:T(8,128)(2,1)S(1)} custom-call(bf16[256,384]{1,0:T(8,128)(2,1)} %q_hbm.1, bf16[256,384]{1,0:T(8,128)(2,1)} %k_hbm.1, bf16[256,384]{1,0:T(8,128)(2,1)} %v_hbm.1, s32[1,12]{1,0:T(1,128)} %bitcast.11, bf16[64,3072]{1,0:T(8,128)(2,1)} %res_hbm.1, bf16[384,3072]{1,0:T(8,128)(2,1)} %w_hbm.1, f32[1,3072]{1,0:T(1,128)} %bitcast.7, ...), custom_call_target="tpu_custom_call" | custom-call | tf_op jit(solution)/shard_map/pallas_call | solution.py:588
  44.1 0.7 %copy.14 = bf16[4,64,512]{2,1,0:T(8,128)(2,1)} copy(bf16[4,64,512]{2,1,0:T(8,128)(2,1)S(1)} %shard_map.118) | data formatting | bytes 524288

commit v6 on v5

--- a/solution.py
+++ b/solution.py
@@ -275,17 +275,18 @@
         loads[h].wait()
     pl.semaphore_wait(barrier, greeted)
 
-    for h in range(HIGH):
-
-        @pl.when(z < 3)
-        def _():
-            up(h).start()
-
-        for far in kinds(h):
+    for far in (2, 0, 1):
+        for h in SIDE if far == 2 else range(HIGH):
 
             @pl.when(asks[far])
             def _():
                 ask(far, h).start()
+
+    for h in range(HIGH):
+
+        @pl.when(z < 3)
+        def _():
+            up(h).start()
 
         if h not in SIDE:
 
@@ -348,17 +349,6 @@
     for h in range(HIGH):
         attend(h, kz[0, h, 0], kz[0, h, 1], 0)
 
-    for h in range(HIGH):
-
-        @pl.when(z >= 1)
-        def _():
-            up(h).wait_recv()
-            lower_across(h).start()
-            attend(h, kz[1, h, 0], kz[1, h, 1], 2)
-
-    for h in SIDE:
-        help_with(2, h, ((kz[0, h, 0], kz[0, h, 1], 1),))
-
     wide[...] = jnp.zeros_like(wide)
     for a in range(2):
         for b in range(2):
@@ -371,8 +361,17 @@
                         tap = (t * 3 + i) * 3 + j
                         wide[a * 2 + b, row : row + LC, :] = dkv[tap * LC : (tap + 1) * LC, :]
 
-    for h in range(HIGH):
-
+    for h in SIDE:
+        help_with(2, h, ((kz[0, h, 0], kz[0, h, 1], 1),))
+
+    def from_below(h):
+        @pl.when(z >= 1)
+        def _():
+            up(h).wait_recv()
+            lower_across(h).start()
+            attend(h, kz[1, h, 0], kz[1, h, 1], 2)
+
+    def from_beside(h):
         @pl.when(z >= 1)
         def _():
             arrived(x, h)
@@ -380,6 +379,12 @@
             help_with(0, h, (lower, (kz[1, h, 0], kz[1, h, 1], 4)))
             help_with(1, h, ((lower[0], lower[1], 5),))
             attend(h, kx[x, h, 0], kx[x, h, 1], 1 + 2 * x)
+
+    for h in range(HIGH):
+        from_below(h)
+        if h:
+            from_beside(h - 1)
+    from_beside(HIGH - 1)
 
     for h in range(HIGH):
         if h in SIDE:

time: 45 us -> 43.6 us (0.969)
  Pallas kernels: 44.1 us -> 42.7 us
    pallas_call x1, Pallas kernels: 44.1 us -> 42.7 us  [fused(): pl.pallas_call(fused_kernel, out_shape=pltpu.VMEM((4, 2 * PW, outputs), b...]
where the time goes in v6:
time: 43.6 us; the launch traced here: 43.4 us
  Pallas kernels  42.7 us (98%)
  local copies, waits for them, and re-layouts  0.71 us (2%)
    pallas_call x1, Pallas kernels, fused(): pl.pallas_call(fused_kernel, out_shape=pltpu.VMEM((4, 2 * PW, outputs), b...  42.7 us

profile of v6, /device:TPU:23, one launch (start us, length us, event | category | flops | bytes accessed | tf_op | source)
XLA Modules:
  0.0 43.4 jit_solution(10722448158565868462)
XLA Ops:
  0.0 42.7 %shard_map.118 = bf16[4,64,512]{2,1,0:T(8,128)(2,1)S(1)} custom-call(bf16[256,384]{1,0:T(8,128)(2,1)} %q_hbm.1, bf16[256,384]{1,0:T(8,128)(2,1)} %k_hbm.1, bf16[256,384]{1,0:T(8,128)(2,1)} %v_hbm.1, s32[1,12]{1,0:T(1,128)} %bitcast.11, bf16[64,3072]{1,0:T(8,128)(2,1)} %res_hbm.1, bf16[384,3072]{1,0:T(8,128)(2,1)} %w_hbm.1, f32[1,3072]{1,0:T(1,128)} %bitcast.7, ...), custom_call_target="tpu_custom_call" | custom-call | tf_op jit(solution)/shard_map/pallas_call | solution.py:593
  42.7 0.7 %copy.14 = bf16[4,64,512]{2,1,0:T(8,128)(2,1)} copy(bf16[4,64,512]{2,1,0:T(8,128)(2,1)S(1)} %shard_map.118) | data formatting | bytes 524288

commit v7 on v6

--- a/solution.py
+++ b/solution.py
@@ -156,7 +156,7 @@
 
 
 HIGH = 3
-CHUNKS = 6
+CHUNKS = 4
 STEPS = (2, 4, 1)
 SIDE = (1, 2)
 LOG2_E = 1.4426950408889634
@@ -284,7 +284,7 @@
 
     for h in range(HIGH):
 
-        @pl.when(z < 3)
+        @pl.when((z < 3) & ((z == 0) | (h == 0)))
         def _():
             up(h).start()
 
@@ -369,6 +369,12 @@
         def _():
             up(h).wait_recv()
             lower_across(h).start()
+            if h < HIGH - 1:
+
+                @pl.when(z < 3)
+                def _():
+                    up(h + 1).start()
+
             attend(h, kz[1, h, 0], kz[1, h, 1], 2)
 
     def from_beside(h):
@@ -443,12 +449,10 @@
 
     for c in range(CHUNKS):
         share(1 - hd, c)
-        if c >= 2:
-            pass_on(c - 2)
-    pass_on(CHUNKS - 2)
-    pass_on(CHUNKS - 1)
     for c in range(CHUNKS):
         share(hd, c)
+    for c in range(CHUNKS):
+        pass_on(c)
     for load in loads[HIGH + 3 :]:
         load.wait()
     for c in range(CHUNKS):

time: 43.6 us -> 44.8 us (1.028)
  Pallas kernels: 42.7 us -> 44 us
    pallas_call x1, Pallas kernels: 42.7 us -> 44 us  [fused(): pl.pallas_call(fused_kernel, out_shape=pltpu.VMEM((4, 2 * PW, outputs), b...]
where the time goes in v7:
time: 44.8 us; the launch traced here: 44.7 us
  Pallas kernels  44 us (98%)
  local copies, waits for them, and re-layouts  0.71 us (2%)
    pallas_call x1, Pallas kernels, fused(): pl.pallas_call(fused_kernel, out_shape=pltpu.VMEM((4, 2 * PW, outputs), b...  44 us

profile of v7, /device:TPU:23, one launch (start us, length us, event | category | flops | bytes accessed | tf_op | source)
XLA Modules:
  0.0 44.7 jit_solution(7845574499621303540)
XLA Ops:
  0.0 44.0 %shard_map.118 = bf16[4,64,512]{2,1,0:T(8,128)(2,1)S(1)} custom-call(bf16[256,384]{1,0:T(8,128)(2,1)} %q_hbm.1, bf16[256,384]{1,0:T(8,128)(2,1)} %k_hbm.1, bf16[256,384]{1,0:T(8,128)(2,1)} %v_hbm.1, s32[1,12]{1,0:T(1,128)} %bitcast.11, bf16[64,3072]{1,0:T(8,128)(2,1)} %res_hbm.1, bf16[384,3072]{1,0:T(8,128)(2,1)} %w_hbm.1, f32[1,3072]{1,0:T(1,128)} %bitcast.7, ...), custom_call_target="tpu_custom_call" | custom-call | tf_op jit(solution)/shard_map/pallas_call | solution.py:597
  44.0 0.7 %copy.14 = bf16[4,64,512]{2,1,0:T(8,128)(2,1)} copy(bf16[4,64,512]{2,1,0:T(8,128)(2,1)S(1)} %shard_map.118) | data formatting | bytes 524288

commit v8 on v6

--- a/solution.py
+++ b/solution.py
@@ -309,8 +309,9 @@
         )
         return jnp.sum(weights, axis=0, keepdims=True), mixed
 
-    def attend(h, key, value, distance):
-        scores = scored(qv[h], key)
+    def attend(h, key, value, distance, scores=None):
+        if scores is None:
+            scores = scored(qv[h], key)
         highest = jnp.max(scores, axis=0, keepdims=True)
         if isinstance(distance, int) and distance == 0:
             total[h], acc[h] = weighed(scores, -highest, value)
@@ -324,23 +325,25 @@
             acc[h] = acc[h] * shrink + mixed
             top[h] = newest
 
+    def answered(far, h, scores, blocks):
+        newest = jnp.full((1, slab), -1e30, jnp.float32)
+        for each, (_, _, distance) in zip(scores, blocks):
+            highest = jnp.max(each, axis=0, keepdims=True)
+            newest = jnp.maximum(newest, jnp.where(visible(h, distance), highest, -1e30))
+        added, mixed = 0.0, 0.0
+        for each, (_, value, distance) in zip(scores, blocks):
+            part_of = weighed(each, jnp.where(visible(h, distance), -newest, -1e30), value)
+            added, mixed = added + part_of[0], mixed + part_of[1]
+        added = jnp.where(added > 0.0, added, 1.0)
+        mixed_out[far, h] = (mixed / added).astype(jnp.bfloat16)
+        level_out[far, h] = jnp.broadcast_to(newest + jnp.log2(added), (8, slab))
+
     def help_with(far, h, blocks):
         @pl.when(helps[far])
         def _():
             ask(far, h).wait_recv()
             query = asked[far, h]
-            newest, scores = jnp.full((1, slab), -1e30, jnp.float32), []
-            for key, _, distance in blocks:
-                scores.append(scored(query, key))
-                highest = jnp.max(scores[-1], axis=0, keepdims=True)
-                newest = jnp.maximum(newest, jnp.where(visible(h, distance), highest, -1e30))
-            added, mixed = 0.0, 0.0
-            for each, (_, value, distance) in zip(scores, blocks):
-                part_of = weighed(each, jnp.where(visible(h, distance), -newest, -1e30), value)
-                added, mixed = added + part_of[0], mixed + part_of[1]
-            added = jnp.where(added > 0.0, added, 1.0)
-            mixed_out[far, h] = (mixed / added).astype(jnp.bfloat16)
-            level_out[far, h] = jnp.broadcast_to(newest + jnp.log2(added), (8, slab))
+            answered(far, h, [scored(query, key) for key, _, _ in blocks], blocks)
             for copy in answer(far, h):
                 copy.start()
 
@@ -375,9 +378,26 @@
         @pl.when(z >= 1)
         def _():
             arrived(x, h)
-            lower = (kx[x, h, 0], kx[x, h, 1], 3 + 2 * x)
-            help_with(0, h, (lower, (kz[1, h, 0], kz[1, h, 1], 4)))
-            help_with(1, h, ((lower[0], lower[1], 5),))
+
+        @pl.when(helps[0])
+        def _():
+            ask(0, h).wait_recv()
+            query, key, value = asked[0, h], kx[x, h, 0], kx[x, h, 1]
+            mine = scored(qv[h], key)
+            answered(
+                0, h, [scored(query, key), scored(query, kz[1, h, 0])],
+                ((key, value, 3 + 2 * x), (None, kz[1, h, 1], 4)),
+            )
+            attend(h, key, value, 1 + 2 * x, mine)
+            for copy in answer(0, h):
+                copy.start()
+
+        @pl.when(helps[1])
+        def _():
+            help_with(1, h, ((kx[0, h, 0], kx[0, h, 1], 5),))
+
+        @pl.when(z == 3)
+        def _():
             attend(h, kx[x, h, 0], kx[x, h, 1], 1 + 2 * x)
 
     for h in range(HIGH):

time: 43.6 us -> 43.5 us (level)
  no operation moved by 1% of the time
where the time goes in v8:
time: 43.5 us; the launch traced here: 43.3 us
  Pallas kernels  42.5 us (98%)
  local copies, waits for them, and re-layouts  0.71 us (2%)
    pallas_call x1, Pallas kernels, fused(): pl.pallas_call(fused_kernel, out_shape=pltpu.VMEM((4, 2 * PW, outputs), b...  42.5 us

profile of v8, /device:TPU:23, one launch (start us, length us, event | category | flops | bytes accessed | tf_op | source)
XLA Modules:
  0.0 43.3 jit_solution(3294940831161227857)
XLA Ops:
  0.0 42.5 %shard_map.118 = bf16[4,64,512]{2,1,0:T(8,128)(2,1)S(1)} custom-call(bf16[256,384]{1,0:T(8,128)(2,1)} %q_hbm.1, bf16[256,384]{1,0:T(8,128)(2,1)} %k_hbm.1, bf16[256,384]{1,0:T(8,128)(2,1)} %v_hbm.1, s32[1,12]{1,0:T(1,128)} %bitcast.11, bf16[64,3072]{1,0:T(8,128)(2,1)} %res_hbm.1, bf16[384,3072]{1,0:T(8,128)(2,1)} %w_hbm.1, f32[1,3072]{1,0:T(1,128)} %bitcast.7, ...), custom_call_target="tpu_custom_call" | custom-call | tf_op jit(solution)/shard_map/pallas_call | solution.py:613
  42.5 0.7 %copy.14 = bf16[4,64,512]{2,1,0:T(8,128)(2,1)} copy(bf16[4,64,512]{2,1,0:T(8,128)(2,1)S(1)} %shard_map.118) | data formatting | bytes 524288
